TPU v7x, 32 devices: a whole 2x2x4 slice. The times are simulated.
32 devices in a mesh: row: 4 (over y, x), col: 8 (over z, core).
Axes of the slice: x: 2, y: 2, z: 4, core: 2. Of those that a mesh axis runs over, the one named last changes fastest.
Arguments:
- inputs: float32 [8, 1024, 2048], P('col', 'row'), may hold values from -6 to 6
- cotangent: float32 [8, 1024, 2048], P('col', 'row'), may hold values from -6 to 6
- image_starts: int32 [8, 2], P('col'), may hold values from 0 to 768, as said below
- owners: int32 [16], replicated, may hold values from 0 to 7, as said below
- query_master: float32 [4096, 3, 2048], P('col', None, 'row'), may hold values from -0.125 to 0.125
- query_first: float32 [4096, 3, 2048], P('col', None, 'row')
- query_second: float32 [4096, 3, 2048], P('col', None, 'row'), may hold values from 8192 to 32768
- output_master: float32 [4096, 2048], P('col', 'row'), may hold values from -1 to 1
- output_first: float32 [4096, 2048], P('col', 'row')
- output_second: float32 [4096, 2048], P('col', 'row'), may hold values from 128 to 512
- gate_master: float32 [4096, 2, 5632], P('col', None, 'row'), may hold values from -0.125 to 0.125
- gate_first: float32 [4096, 2, 5632], P('col', None, 'row')
- gate_second: float32 [4096, 2, 5632], P('col', None, 'row'), may hold values from 1024 to 4096
- down_master: float32 [4096, 5632], P('col', 'row'), may hold values from -0.078125 to 0.078125
- down_first: float32 [4096, 5632], P('col', 'row')
- down_second: float32 [4096, 5632], P('col', 'row'), may hold values from 2048 to 8192
- vector_master: float32 [4096, 7], P('col'), may hold values from -0.5 to 1.4
- vector_first: float32 [4096, 7], P('col')
- vector_second: float32 [4096, 7], P('col'), may hold values from 8192 to 32768
Outputs:
- layer_out: float32 [8, 1024, 2048], P('col', 'row')
- input_grad: float32 [8, 1024, 2048], P('col', 'row')
- query_master_new: float32 [4096, 3, 2048], P('col', None, 'row')
- query_first_new: float32 [4096, 3, 2048], P('col', None, 'row')
- query_second_new: float32 [4096, 3, 2048], P('col', None, 'row')
- output_master_new: float32 [4096, 2048], P('col', 'row')
- output_first_new: float32 [4096, 2048], P('col', 'row')
- output_second_new: float32 [4096, 2048], P('col', 'row')
- gate_master_new: float32 [4096, 2, 5632], P('col', None, 'row')
- gate_first_new: float32 [4096, 2, 5632], P('col', None, 'row')
- gate_second_new: float32 [4096, 2, 5632], P('col', None, 'row')
- down_master_new: float32 [4096, 5632], P('col', 'row')
- down_first_new: float32 [4096, 5632], P('col', 'row')
- down_second_new: float32 [4096, 5632], P('col', 'row')
- vector_master_new: float32 [4096, 7], P('col')
- vector_first_new: float32 [4096, 7], P('col')
- vector_second_new: float32 [4096, 7], P('col')
Inputs may be any that keep to these rules, and one draw needn't show every extreme that they name: `image_starts`: in each sequence the 2 image blocks of 256 positions do not intersect; block k lies within positions k * 512 to (k + 1) * 512 - 1. `owners`: each index of col owns 1 to 4 blocks, and one owns exactly 4.
All inputs are finite; a program needn't handle non-finite values.
Results may differ from a plain program's by a relative error of at most 0.023.
Values may be sent and summed in bfloat16 or wider, within the bound.
No kernel may reach another device: no remote copies, remote signals or barrier semaphores. Data moves between devices by JAX's collectives and lax.ppermute only.
A program may use at most 256 MiB of HBM per device.

v0:
```python
import math

import jax
import jax.numpy as jnp
from jax import lax
from jax.sharding import PartitionSpec as P

D = 2048
HEAD_DIM = 64
FF = 5632
ROT = 16
SEQ = 1024
IMG = 256
STEP = 5
CAP = 4


NORM_EPSILON = 1e-05
ADAM_EPSILON = 1e-08
MOMENT_DECAY = 0.5
WEIGHT_DECAY = 0.1
ROTARY_BASE = 10000.0
MASKED_SCORE = -1e30


def owner_slots(owners):
    block_count = owners.shape[0]
    block_order = jnp.arange(block_count, dtype=jnp.int32)
    before = (owners[:, None] == owners[None, :]) & (block_order[None, :] < block_order[:, None])
    return owners * CAP + jnp.sum(before.astype(jnp.int32), axis=1)


def slot_sources(slot_of, slot_count):
    matches = slot_of[None, :] == jnp.arange(slot_count, dtype=jnp.int32)[:, None]
    filled = jnp.any(matches, axis=1)
    numbers = jnp.arange(slot_of.shape[0], dtype=jnp.int32)
    source = jnp.sum(jnp.where(matches, numbers[None, :], 0), axis=1)
    return (source, filled)


def unpack(gathered, slot_of, block_rows):
    shaped = gathered.reshape((-1, block_rows) + gathered.shape[1:])
    return jnp.take(shaped, slot_of, axis=0).reshape((-1,) + gathered.shape[1:])


def own_blocks(gradient, own_source, block_rows):
    shaped = gradient.reshape((-1, block_rows) + gradient.shape[1:])
    return jnp.take(shaped, own_source, axis=0).reshape((-1,) + gradient.shape[1:])


def normalize(values):
    center = jnp.mean(values, axis=-1, keepdims=True)
    spread = jnp.mean(values * values, axis=-1, keepdims=True) - center * center
    inverse = lax.rsqrt(spread + NORM_EPSILON)
    return ((values - center) * inverse, inverse)


def norm_back(upstream, plain_rows, inverse, gain_row):
    scaled = upstream * gain_row
    return inverse * (
        scaled
        - jnp.mean(scaled, axis=-1, keepdims=True)
        - plain_rows * jnp.mean(scaled * plain_rows, axis=-1, keepdims=True)
    )


def rotary_tables(seq_len):
    half_rot = ROT // 2
    frequency = ROTARY_BASE ** (-2.0 * jnp.arange(half_rot, dtype=jnp.float32) / ROT)
    angles = jnp.arange(seq_len, dtype=jnp.float32)[:, None] * frequency[None, :]
    return (jnp.cos(angles), jnp.sin(angles))


def rotate(values, cosine_table, sine_table):
    half_rot = ROT // 2
    first_half = values[..., :half_rot]
    second_half = values[..., half_rot:ROT]
    cosine_part = cosine_table[:, None, :]
    sine_part = sine_table[:, None, :]
    return jnp.concatenate(
        [
            first_half * cosine_part - second_half * sine_part,
            second_half * cosine_part + first_half * sine_part,
            values[..., ROT:],
        ],
        axis=-1,
    )


def rotate_back(values, cosine_table, sine_table):
    half_rot = ROT // 2
    first_half = values[..., :half_rot]
    second_half = values[..., half_rot:ROT]
    cosine_part = cosine_table[:, None, :]
    sine_part = sine_table[:, None, :]
    return jnp.concatenate(
        [
            first_half * cosine_part + second_half * sine_part,
            second_half * cosine_part - first_half * sine_part,
            values[..., ROT:],
        ],
        axis=-1,
    )


def block_ids(starts, seq_len):
    positions = jnp.arange(seq_len, dtype=jnp.int32)
    inside = (positions[None, :] >= starts[:, None]) & (positions[None, :] < starts[:, None] + IMG)
    numbers = jnp.arange(1, starts.shape[0] + 1, dtype=jnp.int32)
    return jnp.sum(jnp.where(inside, numbers[:, None], 0), axis=0)


def adam_step(master, first_state, second_state, gradient, keep_rows, rate):
    new_first = MOMENT_DECAY * first_state + (1.0 - MOMENT_DECAY) * gradient
    new_second = MOMENT_DECAY * second_state + (1.0 - MOMENT_DECAY) * gradient * gradient
    correction = 1.0 - MOMENT_DECAY**STEP
    direction = new_first / correction / (jnp.sqrt(new_second / correction) + ADAM_EPSILON)
    new_master = master - rate * (direction + WEIGHT_DECAY * master)
    keep_mask = keep_rows.reshape(keep_rows.shape + (1,) * (master.ndim - 1))
    return (
        jnp.where(keep_mask, new_master, master),
        jnp.where(keep_mask, new_first, first_state),
        jnp.where(keep_mask, new_second, second_state),
    )


def step_rates():
    return (
        2.0 / math.sqrt(D),
        2.0 / math.sqrt(D * 16 // SEQ),
        2.0 / math.sqrt(D),
        2.0 / math.sqrt(FF),
        0.5,
    )


def local(
    inputs,
    cotangent,
    image_starts,
    owners,
    query_master,
    query_first,
    query_second,
    output_master,
    output_first,
    output_second,
    gate_master,
    gate_first,
    gate_second,
    down_master,
    down_first,
    down_second,
    vector_master,
    vector_first,
    vector_second,
):
    columns = lax.axis_size("col")
    col_index = lax.axis_index("col")
    row_index = lax.axis_index("row")
    block_rows = D // owners.shape[0]
    slot_of = owner_slots(owners)
    source, filled = slot_sources(slot_of, CAP * columns)
    shared = (
        lax.all_gather(query_master.astype(jnp.bfloat16), "col", axis=0, tiled=True),
        lax.all_gather(output_master.astype(jnp.bfloat16), "col", axis=0, tiled=True),
        lax.all_gather(gate_master.astype(jnp.bfloat16), "col", axis=0, tiled=True),
        lax.all_gather(down_master.astype(jnp.bfloat16), "col", axis=0, tiled=True),
        lax.all_gather(vector_master.astype(jnp.bfloat16), "col", axis=0, tiled=True),
    )
    w_query = unpack(shared[0], slot_of, block_rows)
    w_output = unpack(shared[1], slot_of, block_rows)
    w_gate = unpack(shared[2], slot_of, block_rows)
    w_down = unpack(shared[3], slot_of, block_rows)
    vectors = unpack(shared[4], slot_of, block_rows).astype(jnp.float32)
    local_in = inputs[0]
    width = local_in.shape[1]
    head_cols = w_query.shape[2]
    local_heads = head_cols // HEAD_DIM
    score_scale = 1.0 / math.sqrt(HEAD_DIM)
    qkv_bias = lax.dynamic_slice_in_dim(vectors[:, 4:7], row_index * head_cols, head_cols, 0).T
    plain_one, inverse_one = normalize(local_in)
    normed_one = (plain_one * vectors[:, 0] + vectors[:, 1]).astype(jnp.bfloat16)
    rows_one = lax.all_gather(normed_one, "row", axis=0, tiled=True)
    seq_len = rows_one.shape[0]
    mixed_proj = (
        jnp.einsum("td,djh->tjh", rows_one, w_query, preferred_element_type=jnp.float32)
        + qkv_bias[None]
    )
    cosine_table, sine_table = rotary_tables(seq_len)
    queries = rotate(
        mixed_proj[:, 0].reshape(seq_len, local_heads, HEAD_DIM), cosine_table, sine_table
    ).astype(jnp.bfloat16)
    key_rows = rotate(
        mixed_proj[:, 1].reshape(seq_len, local_heads, HEAD_DIM), cosine_table, sine_table
    ).astype(jnp.bfloat16)
    value_rows = mixed_proj[:, 2].reshape(seq_len, local_heads, HEAD_DIM).astype(jnp.bfloat16)
    labels = block_ids(image_starts[0], seq_len)
    block_size = min(512, seq_len)
    block_count = seq_len // block_size
    positions = jnp.arange(seq_len, dtype=jnp.int32)

    def scores_at(first_row):
        row_pos = first_row + jnp.arange(block_size, dtype=jnp.int32)
        row_label = lax.dynamic_slice_in_dim(labels, first_row, block_size, 0)
        allowed = (positions[None, :] <= row_pos[:, None]) | (
            row_label[:, None] == labels[None, :]
        ) & (row_label[:, None] > 0)
        query_rows = lax.dynamic_slice_in_dim(queries, first_row, block_size, 0)
        raw_scores = (
            jnp.einsum("qhe,khe->hqk", query_rows, key_rows, preferred_element_type=jnp.float32)
            * score_scale
        )
        return (jnp.where(allowed[None], raw_scores, MASKED_SCORE), query_rows)

    def forward_block(block_index):
        scores, query_rows = scores_at(block_index * block_size)
        row_peak = jnp.max(scores, axis=-1, keepdims=True)
        powers = jnp.exp(scores - row_peak)
        row_total = jnp.sum(powers, axis=-1, keepdims=True)
        weights = (powers / row_total).astype(jnp.bfloat16)
        output = jnp.einsum("hqk,khe->qhe", weights, value_rows, preferred_element_type=jnp.float32)
        return (output, (row_peak + jnp.log(row_total))[..., 0])

    output_blocks, log_totals = lax.map(forward_block, jnp.arange(block_count, dtype=jnp.int32))
    attended = output_blocks.reshape(seq_len, head_cols).astype(jnp.bfloat16)
    picked_rows = attended
    middle = local_in + lax.psum_scatter(
        jnp.einsum("th,dh->td", picked_rows, w_output, preferred_element_type=jnp.float32),
        "row",
        scatter_dimension=0,
        tiled=True,
    )
    plain_two, inverse_two = normalize(middle)
    normed_two = (plain_two * vectors[:, 2] + vectors[:, 3]).astype(jnp.bfloat16)
    rows_two = lax.all_gather(normed_two, "row", axis=0, tiled=True)
    gate_up = jnp.einsum("td,djf->tjf", rows_two, w_gate, preferred_element_type=jnp.float32)
    gate_part = gate_up[:, 0]
    up_part = gate_up[:, 1]
    gate_sigmoid = jax.nn.sigmoid(gate_part)
    activated = gate_part * gate_sigmoid
    hidden = (activated * up_part).astype(jnp.bfloat16)
    picked_rows = hidden
    layer_out = middle + lax.psum_scatter(
        jnp.einsum("tf,df->td", picked_rows, w_down, preferred_element_type=jnp.float32).astype(
            jnp.bfloat16
        ),
        "row",
        scatter_dimension=0,
        tiled=True,
    ).astype(jnp.float32)
    upstream = cotangent[0]
    rows_grad = lax.all_gather(upstream.astype(jnp.bfloat16), "row", axis=0, tiled=True)
    hidden_grad = jnp.einsum("td,df->tf", rows_grad, w_down, preferred_element_type=jnp.float32)
    down_grad = jnp.einsum("tf,td->df", hidden, rows_grad, preferred_element_type=jnp.float32)
    gate_grad = hidden_grad * up_part * gate_sigmoid * (1.0 + gate_part * (1.0 - gate_sigmoid))
    up_grad = hidden_grad * activated
    gate_up_grad = jnp.stack([gate_grad, up_grad], axis=1).astype(jnp.bfloat16)
    gate_weight_grad = jnp.einsum(
        "td,tjf->djf", rows_two, gate_up_grad, preferred_element_type=jnp.float32
    )
    picked_rows = gate_up_grad
    normed_two_grad = lax.psum_scatter(
        jnp.einsum("tjf,djf->td", picked_rows, w_gate, preferred_element_type=jnp.float32),
        "row",
        scatter_dimension=0,
        tiled=True,
    )
    middle_grad = upstream + norm_back(normed_two_grad, plain_two, inverse_two, vectors[:, 2])
    rows_mid = lax.all_gather(middle_grad.astype(jnp.bfloat16), "row", axis=0, tiled=True)
    attended_grad = jnp.einsum(
        "td,dh->th", rows_mid, w_output, preferred_element_type=jnp.float32
    ).astype(jnp.bfloat16)
    output_grad = jnp.einsum("th,td->dh", attended, rows_mid, preferred_element_type=jnp.float32)
    head_grad = attended_grad.reshape(seq_len, local_heads, HEAD_DIM)

    def backward_block(running, block_index):
        key_total, value_total = running
        first_row = block_index * block_size
        scores, query_rows = scores_at(first_row)
        probabilities = jnp.exp(scores - log_totals[block_index][..., None])
        row_grad = lax.dynamic_slice_in_dim(head_grad, first_row, block_size, 0)
        prob_grad = jnp.einsum(
            "qhe,khe->hqk", row_grad, value_rows, preferred_element_type=jnp.float32
        )
        inner = jnp.sum(prob_grad * probabilities, axis=-1, keepdims=True)
        score_grad = (probabilities * (prob_grad - inner)).astype(jnp.bfloat16)
        query_grad = (
            jnp.einsum("hqk,khe->qhe", score_grad, key_rows, preferred_element_type=jnp.float32)
            * score_scale
        )
        key_total = (
            key_total
            + jnp.einsum("hqk,qhe->khe", score_grad, query_rows, preferred_element_type=jnp.float32)
            * score_scale
        )
        value_total = value_total + jnp.einsum(
            "hqk,qhe->khe",
            probabilities.astype(jnp.bfloat16),
            row_grad,
            preferred_element_type=jnp.float32,
        )
        return ((key_total, value_total), query_grad)

    empty_heads = jnp.zeros((seq_len, local_heads, HEAD_DIM), jnp.float32)
    (key_grad, value_grad), query_blocks = lax.scan(
        backward_block, (empty_heads, empty_heads), jnp.arange(block_count, dtype=jnp.int32)
    )
    query_grad = query_blocks.reshape(seq_len, local_heads, HEAD_DIM)
    mixed_grad = jnp.stack(
        [
            rotate_back(query_grad, cosine_table, sine_table).reshape(seq_len, head_cols),
            rotate_back(key_grad, cosine_table, sine_table).reshape(seq_len, head_cols),
            value_grad.reshape(seq_len, head_cols),
        ],
        axis=1,
    ).astype(jnp.bfloat16)
    bias_grad = jnp.sum(mixed_grad, axis=0, dtype=jnp.float32)
    query_weight_grad = jnp.einsum(
        "td,tjh->djh", rows_one, mixed_grad, preferred_element_type=jnp.float32
    )
    picked_rows = mixed_grad
    normed_one_grad = lax.psum_scatter(
        jnp.einsum("tjh,djh->td", picked_rows, w_query, preferred_element_type=jnp.float32).astype(
            jnp.bfloat16
        ),
        "row",
        scatter_dimension=0,
        tiled=True,
    ).astype(jnp.float32)
    input_grad = middle_grad + norm_back(normed_one_grad, plain_one, inverse_one, vectors[:, 0])
    norm_grads = jnp.stack(
        [
            jnp.sum(normed_one_grad * plain_one, axis=0),
            jnp.sum(normed_one_grad, axis=0),
            jnp.sum(normed_two_grad * plain_two, axis=0),
            jnp.sum(normed_two_grad, axis=0),
        ],
        axis=1,
    )
    placed = lax.dynamic_update_slice_in_dim(
        jnp.zeros((width, 3), jnp.float32), bias_grad.T, row_index * head_cols, 0
    )
    vector_grad = lax.psum(
        jnp.concatenate([norm_grads, placed], axis=1).astype(jnp.bfloat16), "row"
    )
    own_filled = lax.dynamic_slice_in_dim(filled, col_index * CAP, CAP, 0)
    own_source = lax.dynamic_slice_in_dim(source, col_index * CAP, CAP, 0)
    summed = (
        lax.psum(query_weight_grad.astype(jnp.bfloat16), "col").astype(jnp.float32),
        lax.psum(output_grad.astype(jnp.bfloat16), "col").astype(jnp.float32),
        lax.psum(gate_weight_grad.astype(jnp.bfloat16), "col").astype(jnp.float32),
        lax.psum(down_grad.astype(jnp.bfloat16), "col").astype(jnp.float32),
        lax.psum(vector_grad, "col").astype(jnp.float32),
    )
    owned_grads = tuple((own_blocks(whole_grad, own_source, block_rows) for whole_grad in summed))
    keep_rows = jnp.repeat(own_filled, block_rows)
    masters = (query_master, output_master, gate_master, down_master, vector_master)
    firsts = (query_first, output_first, gate_first, down_first, vector_first)
    seconds = (query_second, output_second, gate_second, down_second, vector_second)
    rates = step_rates()
    updated = [
        adam_step(
            masters[kind_index],
            firsts[kind_index],
            seconds[kind_index],
            owned_grads[kind_index],
            keep_rows,
            rates[kind_index],
        )
        for kind_index in range(5)
    ]
    return (
        layer_out[None],
        input_grad[None],
        updated[0][0],
        updated[0][1],
        updated[0][2],
        updated[1][0],
        updated[1][1],
        updated[1][2],
        updated[2][0],
        updated[2][1],
        updated[2][2],
        updated[3][0],
        updated[3][1],
        updated[3][2],
        updated[4][0],
        updated[4][1],
        updated[4][2],
    )


def solution(mesh):
    return jax.shard_map(
        local,
        mesh=mesh,
        in_specs=(
            P("col", "row", None),
            P("col", "row", None),
            P("col", None),
            P(),
            P("col", None, "row"),
            P("col", None, "row"),
            P("col", None, "row"),
            P("col", "row"),
            P("col", "row"),
            P("col", "row"),
            P("col", None, "row"),
            P("col", None, "row"),
            P("col", None, "row"),
            P("col", "row"),
            P("col", "row"),
            P("col", "row"),
            P("col", None),
            P("col", None),
            P("col", None),
        ),
        out_specs=(
            P("col", "row", None),
            P("col", "row", None),
            P("col", None, "row"),
            P("col", None, "row"),
            P("col", None, "row"),
            P("col", "row"),
            P("col", "row"),
            P("col", "row"),
            P("col", None, "row"),
            P("col", None, "row"),
            P("col", None, "row"),
            P("col", "row"),
            P("col", "row"),
            P("col", "row"),
            P("col", None),
            P("col", None),
            P("col", None),
        ),
        check_vma=False,
    )
```

profile of v0, /device:TPU:0, one launch (start us, length us, event | category | flops | bytes accessed | tf_op | source)
XLA Modules:
  0.0 1877.9 jit_solution(9578994907505694291)
XLA Ops:
  13.1 15.7 all_gather.27
  33.1 27.2 %all-gather.13.cloned.1.call-done = bf16[4096,512]{1,0:T(8,128)(2,1)} async-done(((bf16[512,512]{1,0:T(8,128)(2,1)}), bf16[4096,512]{1,0:T(8,128)(2,1)}) %all-gather.13.cloned.1.call-update) | async-done | bytes 4194320 | tf_op jit(solution)/shard_map/all_gather | solution.py:166
  65.0 113.1 %all-gather.11.cloned.1.call-done = bf16[4096,3,512]{2,0,1:T(8,128)(2,1)} async-done(((bf16[512,3,512]{2,0,1:T(8,128)(2,1)}), bf16[4096,3,512]{2,0,1:T(8,128)(2,1)}) %all-gather.11.cloned.1.call-update) | async-done | bytes 12582928 | tf_op jit(solution)/shard_map/all_gather | solution.py:165
  193.8 37.6 %all-gather.9.cloned.1.call-done = bf16[1024,2048]{1,0:T(8,128)(2,1)} async-done(((bf16[256,2048]{1,0:T(8,128)(2,1)}), bf16[1024,2048]{1,0:T(8,128)(2,1)}) %all-gather.9.cloned.1.call-update) | async-done | bytes 4194320 | tf_op jit(solution)/shard_map/all_gather | solution.py:184
  231.4 10.4 broadcast_add_fusion
  242.9 33.2 %while.28 = (s32[]{:T(128)}, bf16[2,512,8,64]{1,3,2,0:T(8,128)(2,1)}, f32[2,8,512]{2,1,0:T(8,128)}, s32[2]{0:T(128)S(1)}, s32[1024]{0:T(1024)S(1)}, /*index=5*/b...) while((s32[]{:T(128)}, ...), condition=%wide.region_7.8_spmd.clone, body=%wide.region_4.7_spmd.clone.sunk | while | flops 1126167552 | bytes 64896316 | solution.py:225
  295.8 77.0 %reduce-scatter.5.cloned.1.call-done = f32[256,2048]{1,0:T(8,128)} async-done(((f32[1024,2048]{1,0:T(8,128)}), f32[256,2048]{1,0:T(8,128)}) %reduce-scatter.5.cloned.1.call-update) | async-done | bytes 2097168 | tf_op jit(solution)/shard_map/reduce_scatter | solution.py:228
  378.8 104.2 %all-gather.19.cloned.1.call-done = bf16[4096,1408]{1,0:T(8,128)(2,1)} async-done(((bf16[512,1408]{1,0:T(8,128)(2,1)}), bf16[4096,1408]{1,0:T(8,128)(2,1)}) %all-gather.19.cloned.1.call-update) | async-done | bytes 11534352 | tf_op jit(solution)/shard_map/all_gather | solution.py:168
  498.9 187.3 %all-gather.17.cloned.1.call-done = bf16[4096,2,1408]{2,1,0:T(2,128)(2,1)} async-done(((bf16[512,2,1408]{2,1,0:T(2,128)(2,1)}), bf16[4096,2,1408]{2,1,0:T(2,128)(2,1)}) %all-gather.17.cloned.1.call-update) | async-done | bytes 23068688 | tf_op jit(solution)/shard_map/all_gather | solution.py:167
  686.2 32.9 %gather_fusion.3 = bf16[16,128,2,1408]{3,2,1,0:T(2,128)(2,1)} fusion(bf16[32,128,2,1408]{3,2,1,0:T(2,128)(2,1)} %bitcast.296, s32[1024]{0:T(1024)} %copy-done.51), kind=kCustom, calls=%fused_computation.3 | custom fusion | bytes 23068736 | tf_op jit(solution)/shard_map/jit(_take)/gather | solution.py:43
  739.7 18.7 fusion.42
  758.4 36.6 %all-gather.21.cloned.1.call-done = bf16[1024,2048]{1,0:T(8,128)(2,1)} async-done(((bf16[256,2048]{1,0:T(8,128)(2,1)}), bf16[1024,2048]{1,0:T(8,128)(2,1)}) %all-gather.21.cloned.1.call-update) | async-done | bytes 4194320 | tf_op jit(solution)/shard_map/all_gather | solution.py:253
  795.0 15.6 fusion.52
  810.6 16.3 convolution_bitcast_fusion
  830.9 13.4 convolution_convert_fusion.3
  844.4 69.2 %reduce-scatter.9.cloned.1.call-done = f32[256,2048]{1,0:T(8,128)} async-done(((f32[1024,2048]{1,0:T(8,128)}), f32[256,2048]{1,0:T(8,128)}) %reduce-scatter.9.cloned.1.call-update) | async-done | bytes 2097168 | tf_op jit(solution)/shard_map/reduce_scatter | solution.py:263
  916.7 53.0 %reduce-scatter.7.cloned.1.call-done = bf16[256,2048]{1,0:T(8,128)(2,1)} async-done(((bf16[1024,2048]{1,0:T(8,128)(2,1)}), bf16[256,2048]{1,0:T(8,128)(2,1)}) %reduce-scatter.7.cloned.1.call-update) | async-done | bytes 1048592 | tf_op jit(solution)/shard_map/reduce_scatter | solution.py:244
  977.4 51.0 %all-gather.23.cloned.1.call-done = bf16[1024,2048]{1,0:T(8,128)(2,1)} async-done(((bf16[256,2048]{1,0:T(8,128)(2,1)}), bf16[1024,2048]{1,0:T(8,128)(2,1)}) %all-gather.23.cloned.1.call-update) | async-done | bytes 4194320 | tf_op jit(solution)/shard_map/all_gather | solution.py:270
  1033.9 130.6 %while.29 = (s32[]{:T(128)}, f32[1024,8,64]{0,2,1:T(8,128)}, f32[1024,8,64]{0,2,1:T(8,128)}, f32[2,512,8,64]{1,0,3,2:T(2,128)}, s32[2]{0:T(128)S(1)}, /*index=5*...) while((s32[]{:T(128)}, f32[1024,8,64]{0,2,1:T(8,128)}, ...), condition=%wide.region_17.18_spmd.clone, body=%wide.region_15.17_spmd.clone.sunk | while | flops 2727080960 | bytes 200375696 | solution.py:306
  1047.9 10.3 multiply_reduce_fusion.6
  1079.0 19.6 %dynamic_update_slice.26 = f32[2,512,8,64]{1,0,3,2:T(2,128)} dynamic-update-slice(f32[2,512,8,64]{1,0,3,2:T(2,128)} %get-tuple-element.491, f32[1,512,8,64]{1,0,3,2:T(1,128)} %copy.134, s32[]{:T(128)S(6)} %copy.151, s32[]{:T(128)} %constant.159.clone.1..sunk.1, s32[]{:T(128)} %constant.159.clone.1..sunk.1, s32[]{:T(128)} %constant.159.clone.1..sunk.1) | dynamic-update-slice | bytes 2097156 | tf_op jit(solution)/shard_map/while/body/jit(dynamic_update_index_in_dim)/dynamic_update_slice | solution.py:225
  1113.8 10.3 multiply_reduce_fusion.6
  1144.8 19.6 %dynamic_update_slice.26 = f32[2,512,8,64]{1,0,3,2:T(2,128)} dynamic-update-slice(f32[2,512,8,64]{1,0,3,2:T(2,128)} %get-tuple-element.491, f32[1,512,8,64]{1,0,3,2:T(1,128)} %copy.134, s32[]{:T(128)S(6)} %copy.151, s32[]{:T(128)} %constant.159.clone.1..sunk.1, s32[]{:T(128)} %constant.159.clone.1..sunk.1, s32[]{:T(128)} %constant.159.clone.1..sunk.1) | dynamic-update-slice | bytes 2097156 | tf_op jit(solution)/shard_map/while/body/jit(dynamic_update_index_in_dim)/dynamic_update_slice | solution.py:225
  1177.4 10.4 bitcast_convert_fusion
  1187.9 13.2 fusion.30
  1209.2 18.7 convolution_convert_fusion
  1247.8 15.5 psum.46
  1263.3 28.3 %psum.47 = bf16[16,128,7]{1,2,0:T(8,128)(2,1)S(1)} all-reduce(bf16[16,128,7]{1,2,0:T(8,128)(2,1)S(1)} %bitcast.319), channel_id=1, replica_groups=mesh['row'=4,'col'=8] {'col'}, use_global_device_ids=true, to_apply=%region_33.34 | all-reduce | flops 14336 | bytes 57344 | tf_op jit(solution)/shard_map/psum | solution.py:354
  1296.6 450.7 %all-reduce.3.cloned.1.call-done = (bf16[16,128,3,512]{3,1,0,2:T(8,128)(2,1)}, bf16[16,128,512]{2,1,0:T(8,128)(2,1)}, bf16[16,128,2,1408]{3,1,0,2:T(8,128)(2,1)}, bf16[16,128,1408]{2,1,0:T(8,128)(2,1)}) async-done(((bf16[16,128,3,512]{3,1,0,2:T(8,128)(2,1)}, bf16[16,128,512]{2,1,0:T(8,128)(2,1)}, bf16[16,128,2,1408]{3,1,0,2:T(8,128)(2,1)}, bf16[16,128,1408]{2,1,0:T(8,128)(2,1)}), ...) | async-done | bytes 25690128 | tf_op jit(solution)/shard_map/psum | solution.py:350
  1786.6 13.0 reshape.488
  1799.6 11.0 gather_fusion.7
  1839.8 31.5 %broadcast_select_fusion = (f32[512,2,1408]{2,1,0:T(2,128)}, f32[512,2,1408]{2,1,0:T(2,128)}, f32[512,2,1408]{2,1,0:T(2,128)}) fusion(f32[512,2,1408]{2,1,0:T(2,128)S(1)} %bitcast.299, pred[512]{0:T(512)(128)(4,1)S(1)} %get-tuple-element.303, f32[4,128,2,1408]{3,2,1,0:T(2,128)S(1)} %copy.108, pred[512]{0:T(512)(128)(4,1)S(1)} %get-tuple-element.302, ...), kind=kLoop, calls=%fused_computation.83 | loop fusion | flops 25952256 | bytes 40371200 | tf_op jit(solution)/shard_map/jit(_where)/select_n | solution.py:123
  (317 shorter events, 323.6 us)
Async XLA Ops:
  7.2 53.1 %all-gather.13.cloned.1.call-start = ((), (), s32[]{:S(2)}) async-start(), calls=%async_computation.6 | async-start | bytes 4718592 | tf_op jit(solution)/shard_map/all_gather | solution.py:166
  9.5 168.5 %all-gather.11.cloned.1.call-start = ((), (), s32[]{:S(2)}) async-start(), calls=%async_computation.5 | async-start | bytes 14155776 | tf_op jit(solution)/shard_map/all_gather | solution.py:165
  12.8 218.5 %all-gather.9.cloned.1.call-start = ((), (), s32[]{:S(2)}) async-start(), calls=%async_computation.4 | async-start | bytes 5242880 | tf_op jit(solution)/shard_map/all_gather | solution.py:184
  29.0 34.1 %copy-start.52 = (pred[16]{0:T(512)(128)(4,1)}, pred[16]{0:T(512)(128)(4,1)S(1)}, u32[]{:S(2)}) copy-start(pred[16]{0:T(512)(128)(4,1)S(1)} %get-tuple-element.250) | copy-start | bytes 52
  29.6 148.4 %copy-start.51 = (s32[1024]{0:T(1024)}, s32[1024]{0:T(1024)S(1)}, u32[]{:S(2)}) copy-start(s32[1024]{0:T(1024)S(1)} %pad_clamp_fusion.1) | copy-start | bytes 12292
  30.5 159.4 %copy-start.38 = (pred[2048]{0:T(1024)(128)(4,1)}, pred[2048]{0:T(1024)(128)(4,1)S(1)}, u32[]{:S(2)}) copy-start(pred[2048]{0:T(1024)(128)(4,1)S(1)} %broadcast_bitcast_fusion) | copy-start | bytes 6148
  31.2 32.0 %copy-start.36 = (f32[2048,1]{0,1:T(1,128)}, f32[2048,1]{0,1:T(1,128)S(1)}, u32[]{:S(2)}) copy-start(f32[2048,1]{0,1:T(1,128)S(1)} %get-tuple-element.286) | copy-start | bytes 24580
  32.6 340.1 %reduce-scatter.5.cloned.1.call-start = ((), (), s32[]{:S(2)}) async-start(), calls=%async_computation.7 | async-start | bytes 10485760 | tf_op jit(solution)/shard_map/reduce_scatter | solution.py:228
  33.1 209.4 %copy-start.29 = (f32[1024,8]{0,1:T(8,128)}, f32[1024,8]{0,1:T(8,128)S(1)}, u32[]{:S(2)}) copy-start(f32[1024,8]{0,1:T(8,128)S(1)} %get-tuple-element.296) | copy-start | bytes 98308
  33.1 209.4 %copy-start.31 = (f32[1024,8]{0,1:T(8,128)}, f32[1024,8]{0,1:T(8,128)S(1)}, u32[]{:S(2)}) copy-start(f32[1024,8]{0,1:T(8,128)S(1)} %get-tuple-element.297) | copy-start | bytes 98308
  63.2 123.1 %copy-start.12 = (bf16[16,128,512]{2,1,0:T(8,128)(2,1)}, bf16[16,128,512]{2,1,0:T(8,128)(2,1)S(1)}, u32[]{:S(2)}) copy-start(bf16[16,128,512]{2,1,0:T(8,128)(2,1)S(1)} %gather_fusion.2) | copy-start | bytes 6291460
  286.2 196.8 %all-gather.19.cloned.1.call-start = ((), (), s32[]{:S(2)}) async-start(), calls=%async_computation.10 | async-start | bytes 12976128 | tf_op jit(solution)/shard_map/all_gather | solution.py:168
  289.3 83.4 %copy-start.5 = (f32[1,256,2048]{2,1,0:T(8,128)S(1)}, f32[1,256,2048]{2,1,0:T(8,128)}, u32[]{:S(2)}) copy-start(f32[1,256,2048]{2,1,0:T(8,128)} %param.23) | copy-start | bytes 6291460
  289.3 396.9 %all-gather.17.cloned.1.call-start = ((), (), s32[]{:S(2)}) async-start(), calls=%async_computation.9 | async-start | bytes 25952256 | tf_op jit(solution)/shard_map/all_gather | solution.py:167
  295.7 80.4 %copy-start.35 = (f32[2048,1]{0,1:T(1,128)S(1)}, f32[2048,1]{0,1:T(1,128)}, u32[]{:S(2)}) copy-start(f32[2048,1]{0,1:T(1,128)} %get-tuple-element.283) | copy-start | bytes 24580
  295.7 80.4 %copy-start.42 = (f32[2048,1]{0,1:T(1,128)S(1)}, f32[2048,1]{0,1:T(1,128)}, u32[]{:S(2)}) copy-start(f32[2048,1]{0,1:T(1,128)} %get-tuple-element.284) | copy-start | bytes 24580
  295.7 443.9 %all-gather.15.cloned.1.call-start = ((), (), s32[]{:S(2)}) async-start(), calls=%async_computation.8 | async-start | bytes 5242880 | tf_op jit(solution)/shard_map/all_gather | solution.py:236
  377.6 417.4 %all-gather.21.cloned.1.call-start = ((), (), s32[]{:S(2)}) async-start(), calls=%async_computation.12 | async-start | bytes 5242880 | tf_op jit(solution)/shard_map/all_gather | solution.py:253
  378.8 534.8 %reduce-scatter.9.cloned.1.call-start = ((), (), s32[]{:S(2)}) async-start(), calls=%async_computation.13 | async-start | bytes 10485760 | tf_op jit(solution)/shard_map/reduce_scatter | solution.py:263
  827.0 142.7 %reduce-scatter.7.cloned.1.call-start = ((), (), s32[]{:S(2)}) async-start(), calls=%async_computation.11 | async-start | bytes 5242880 | tf_op jit(solution)/shard_map/reduce_scatter | solution.py:244
  844.3 69.3 %copy-start.10 = (f32[256,2048]{1,0:T(8,128)S(1)}, f32[256,2048]{1,0:T(8,128)}, u32[]{:S(2)}) copy-start(f32[256,2048]{1,0:T(8,128)} %copy-done.9) | copy-start | bytes 6291460
  844.3 184.1 %all-gather.23.cloned.1.call-start = ((), (), s32[]{:S(2)}) async-start(), calls=%async_computation.14 | async-start | bytes 5242880 | tf_op jit(solution)/shard_map/all_gather | solution.py:270
  975.5 268.5 %reduce-scatter.11.cloned.1.call-start = ((), (), s32[]{:S(2)}) async-start(), calls=%async_computation.15 | async-start | bytes 5242880 | tf_op jit(solution)/shard_map/reduce_scatter | solution.py:323
  1076.9 21.7 %copy-start.2 = (f32[1024,8,64]{0,2,1:T(8,128)}, f32[1024,8,64]{0,2,1:T(8,128)S(1)}, u32[]{:S(2)}) copy-start(f32[1024,8,64]{0,2,1:T(8,128)S(1)} %bitcast_add_fusion.8) | copy-start | bytes 6291460 | tf_op jit(solution)/shard_map/while
  1173.9 57.9 %copy-start.20 = (bf16[1024,1,512]{2,0,1:T(8,128)(2,1)}, bf16[1024,1,512]{2,0,1:T(8,128)(2,1)S(1)}, u32[]{:S(2)}) copy-start(bf16[1024,1,512]{2,0,1:T(8,128)(2,1)S(1)} %copy.103) | copy-start | bytes 3145732
  1187.8 559.5 %all-reduce.3.cloned.1.call-start = ((), (), s32[]{:S(2)}) async-start(), calls=%async_computation.16 | async-start | bytes 51380224 | tf_op jit(solution)/shard_map/psum | solution.py:350
  1240.9 51.3 %copy-start.41 = (f32[512,7]{0,1:T(8,128)S(1)}, f32[512,7]{0,1:T(8,128)}, u32[]{:S(2)}) copy-start(f32[512,7]{0,1:T(8,128)} %param.39) | copy-start | bytes 43012
  1240.9 51.3 %copy-start.45 = (f32[512,7]{0,1:T(8,128)S(1)}, f32[512,7]{0,1:T(8,128)}, u32[]{:S(2)}) copy-start(f32[512,7]{0,1:T(8,128)} %param.41) | copy-start | bytes 43012
  1240.9 51.3 %copy-start.46 = (f32[512,7]{0,1:T(8,128)S(1)}, f32[512,7]{0,1:T(8,128)}, u32[]{:S(2)}) copy-start(f32[512,7]{0,1:T(8,128)} %param.40) | copy-start | bytes 43012
  1244.0 48.8 %copy-start.18 = (bf16[256,2048]{1,0:T(8,128)(2,1)S(1)}, bf16[256,2048]{1,0:T(8,128)(2,1)}, u32[]{:S(2)}) copy-start(bf16[256,2048]{1,0:T(8,128)(2,1)} %reduce-scatter.11.cloned.1.call-done) | copy-start | bytes 3145732
  1817.9 21.8 %slice-start = ((s8[5767168]{0:T(1024)(128)(4,1)}), s8[4194304]{0:T(1024)(128)(4,1)S(1)}, s32[]{:S(2)}) async-start(s8[5767168]{0:T(1024)(128)(4,1)} %bitcast.291), calls=%async_computation.17 | async-start | bytes 8388608
  1817.9 21.8 %slice-start.2 = ((s8[5767168]{0:T(1024)(128)(4,1)}), s8[4194304]{0:T(1024)(128)(4,1)S(1)}, s32[]{:S(2)}) async-start(s8[5767168]{0:T(1024)(128)(4,1)} %bitcast.298), calls=%async_computation.19 | async-start | bytes 8388608
  (53 other events, 350.1 us)
Sparse Core Ops, SparseCore 0:
  10.2 50.0 all-gather.12
  62.5 115.4 all-gather.10
  180.4 50.8 all-gather.8
  286.3 86.4 reduce-scatter.4
  374.9 108.0 all-gather.18
  485.2 200.9 all-gather.16
  688.8 50.8 all-gather.14
  742.2 52.6 all-gather.20
  827.1 86.4 reduce-scatter.8
  916.9 52.6 reduce-scatter.6
  975.7 52.6 all-gather.22
  1187.9 52.6 reduce-scatter.10
  1244.1 503.1 all-reduce.2
where the time goes:
time: 1890 us; the launch traced here: 1880 us
  waiting for transfers between devices  1210 us (64%)
  matrix products  216 us (11%)
  other arithmetic  187 us (10%)
  local copies, waits for them, and re-layouts  178 us (9%)
  blocking collectives  59.5 us (3%)
    psum x1, waiting for transfers between devices, local(): lax.psum(query_weight_grad.astype(jnp.bfloat16), 'col').astype(jnp.float32)  451 us
    all_gather x1, waiting for transfers between devices, local(): lax.all_gather(gate_master.astype(jnp.bfloat16), 'col', axis=0, tiled=True)  187 us
    all_gather x1, waiting for transfers between devices, local(): lax.all_gather(query_master.astype(jnp.bfloat16), 'col', axis=0, tiled=True)  113 us
    all_gather x1, waiting for transfers between devices, local(): lax.all_gather(down_master.astype(jnp.bfloat16), 'col', axis=0, tiled=True)  104 us
    reduce_scatter x1, waiting for transfers between devices, local(): lax.psum_scatter(jnp.einsum('th,dh->td', picked_rows, w_output, preferred...  77 us
    reduce_scatter x1, waiting for transfers between devices, local(): lax.psum_scatter(jnp.einsum('tjf,djf->td', picked_rows, w_gate, preferred...  69.2 us
    gather x7, local copies, waits for them, and re-layouts, unpack(): return jnp.take(shaped, slot_of, axis=0).reshape((-1,) + gathered.shape[1:])  64.5 us
    select_n x5, other arithmetic, adam_step(): jnp.where(keep_mask, new_second, second_state)  53.8 us
  transfers between devices with their start and end apart: 13, of which 12 were waited for; matrix products, arithmetic and copies ran while one was open for 11% of the time, Pallas kernels for 0%

commit v1 on v0

--- a/solution.py
+++ b/solution.py
@@ -2,7 +2,11 @@
 
 import jax
 import jax.numpy as jnp
+import numpy as np
 from jax import lax
+from jax.experimental import pallas as pl
+from jax.experimental.layout import Layout, with_layout_constraint
+from jax.experimental.pallas import tpu as pltpu
 from jax.sharding import PartitionSpec as P
 
 D = 2048
@@ -14,6 +18,8 @@
 STEP = 5
 CAP = 4
 
+LANES = 128
+MIB = 1 << 20
 
 NORM_EPSILON = 1e-05
 ADAM_EPSILON = 1e-08
@@ -391,9 +397,1208 @@
     )
 
 
+BF16 = jnp.bfloat16
+F32 = jnp.float32
+
+
+def smem():
+    return pl.BlockSpec(memory_space=pltpu.SMEM)
+
+
+def params(mib=32):
+    return pltpu.CompilerParams(vmem_limit_bytes=mib * MIB)
+
+
+def cost(flops, nbytes, powers=0):
+    return pl.CostEstimate(flops=int(flops), bytes_accessed=int(nbytes), transcendentals=int(powers))
+
+
+def lane_block(number):
+    return pl.ds(pl.multiple_of(number * LANES, LANES), LANES)
+
+
+def after(value, *others):
+    return lax.optimization_barrier((value, *others))[0]
+
+
+def pack_query(slabs):
+    kinds, rows, width = slabs.shape
+    block = rows // CAP
+
+    def kernel(in_ref, out_ref):
+        for kind in range(kinds):
+            out_ref[0, :, kind * width : (kind + 1) * width] = in_ref[kind].astype(BF16)
+
+    return pl.pallas_call(
+        kernel,
+        grid=(CAP,),
+        in_specs=[pl.BlockSpec((kinds, block, width), lambda s: (0, s, 0))],
+        out_specs=pl.BlockSpec((1, block, kinds * width), lambda s: (s, 0, 0)),
+        out_shape=jax.ShapeDtypeStruct((CAP, block, kinds * width), BF16),
+        compiler_params=params(),
+        cost_estimate=cost(0, 6 * slabs.size),
+        name="pack_query",
+    )(slabs)
+
+
+def pack_flat(name, master):
+    rows, width = master.shape
+    block = rows // CAP
+
+    def kernel(in_ref, out_ref):
+        out_ref[0] = in_ref[...].astype(BF16)
+
+    return pl.pallas_call(
+        kernel,
+        grid=(CAP,),
+        in_specs=[pl.BlockSpec((block, width), lambda s: (s, 0))],
+        out_specs=pl.BlockSpec((1, block, width), lambda s: (s, 0, 0)),
+        out_shape=jax.ShapeDtypeStruct((CAP, block, width), BF16),
+        compiler_params=params(),
+        cost_estimate=cost(0, 6 * rows * width),
+        name=name,
+    )(master)
+
+
+def gate_lines(values):
+    rows, kinds, width = values.shape
+    split = with_layout_constraint(
+        values.reshape(rows, kinds, width // LANES, LANES), Layout(major_to_minor=(0, 2, 1, 3))
+    )
+    return jnp.transpose(split, (0, 2, 1, 3)).reshape(rows * kinds * width // LANES, LANES)
+
+
+def gate_unlines(lines, shape):
+    rows, kinds, width = shape
+    split = jnp.transpose(lines.reshape(rows, width // LANES, kinds, LANES), (0, 2, 1, 3))
+    return with_layout_constraint(split, Layout(major_to_minor=(0, 2, 1, 3))).reshape(shape)
+
+
+def pack_gate(lines, rows):
+    block = rows // CAP
+    tiles = lines.shape[0] // rows
+
+    def kernel(in_ref, out_ref):
+        for tile in range(tiles):
+            out_ref[0, :, tile * LANES : (tile + 1) * LANES] = in_ref[
+                pl.ds(tile, block, stride=tiles), :
+            ].astype(BF16)
+
+    return pl.pallas_call(
+        kernel,
+        grid=(CAP,),
+        in_specs=[pl.BlockSpec((block * tiles, LANES), lambda s: (s, 0))],
+        out_specs=pl.BlockSpec((1, block, tiles * LANES), lambda s: (s, 0, 0)),
+        out_shape=jax.ShapeDtypeStruct((CAP, block, tiles * LANES), BF16),
+        compiler_params=params(),
+        cost_estimate=cost(0, 6 * lines.size),
+        name="pack_gate",
+    )(lines)
+
+
+def pick_blocks(codes, first, count, sources):
+    shape = sources[0].shape[1:]
+
+    def kernel(code_ref, *refs):
+        ins, out, sems = refs[: len(sources)], refs[-2], refs[-1]
+        for place in range(count):
+            code = code_ref[first + place]
+            index = jnp.bitwise_and(code, 15)
+            origin = lax.shift_right_logical(code, 4)
+            for number, source in enumerate(ins):
+
+                @pl.when(origin == number)
+                def start(source=source, index=index, place=place):
+                    pltpu.make_async_copy(source.at[index], out.at[place], sems.at[place]).start()
+
+        for place in range(count):
+            pltpu.make_async_copy(ins[0].at[0], out.at[place], sems.at[place]).wait()
+
+    moved = count * shape[0] * shape[1]
+    return pl.pallas_call(
+        kernel,
+        in_specs=[smem()] + [pl.BlockSpec(memory_space=pl.ANY)] * len(sources),
+        out_specs=pl.BlockSpec(memory_space=pltpu.VMEM),
+        out_shape=jax.ShapeDtypeStruct((count, *shape), BF16),
+        scratch_shapes=[pltpu.SemaphoreType.DMA((count,))],
+        compiler_params=params(16),
+        cost_estimate=cost(0, 4 * moved),
+        name="pick_blocks",
+    )(codes, *sources)
+
+
+def row_blocks(height, width, first=0):
+    return pl.BlockSpec((height, width), lambda i: (i + first, 0))
+
+
+def whole(height, width):
+    return pl.BlockSpec((height, width), lambda i: (0, 0))
+
+
+NORM_ROWS = 64
+
+
+def statistics(values):
+    center = jnp.mean(values, axis=-1, keepdims=True)
+    spread = jnp.mean(values * values, axis=-1, keepdims=True) - center * center
+    return center, lax.rsqrt(spread + NORM_EPSILON)
+
+
+def order_grad(order, cotangent):
+    rows, width = cotangent.shape
+
+    def kernel(order_ref, in_ref, out_ref):
+        for place in range(width // LANES):
+            out_ref[:, place * LANES : (place + 1) * LANES] = in_ref[
+                :, lane_block(order_ref[place])
+            ].astype(BF16)
+
+    return pl.pallas_call(
+        kernel,
+        grid=(rows // NORM_ROWS,),
+        in_specs=[smem(), row_blocks(NORM_ROWS, width)],
+        out_specs=row_blocks(NORM_ROWS, width),
+        out_shape=jax.ShapeDtypeStruct((rows, width), BF16),
+        compiler_params=params(16),
+        cost_estimate=cost(0, 6 * rows * width),
+        name="order_grad",
+    )(order, cotangent)
+
+
+def norm_one(order, inputs):
+    rows, width = inputs.shape
+
+    def kernel(order_ref, in_ref, out_ref):
+        center, inverse = statistics(in_ref[...])
+        for place in range(width // LANES):
+            span = slice(place * LANES, (place + 1) * LANES)
+            plain = (in_ref[:, lane_block(order_ref[place])] - center) * inverse
+            out_ref[:, span] = plain.astype(BF16)
+
+    return pl.pallas_call(
+        kernel,
+        grid=(rows // NORM_ROWS,),
+        in_specs=[smem(), row_blocks(NORM_ROWS, width)],
+        out_specs=row_blocks(NORM_ROWS, width),
+        out_shape=jax.ShapeDtypeStruct((rows, width), BF16),
+        compiler_params=params(16),
+        cost_estimate=cost(0, 6 * rows * width),
+        name="norm_one",
+    )(order, inputs)
+
+
+def scale_rows(plain, vectors):
+    rows, width = plain.shape
+    tile = 256
+
+    def kernel(in_ref, vec_ref, out_ref):
+        out_ref[...] = (in_ref[...].astype(F32) * vec_ref[0:1, :] + vec_ref[1:2, :]).astype(BF16)
+
+    return pl.pallas_call(
+        kernel,
+        grid=(rows // tile,),
+        in_specs=[row_blocks(tile, width), whole(8, width)],
+        out_specs=row_blocks(tile, width),
+        out_shape=jax.ShapeDtypeStruct((rows, width), BF16),
+        compiler_params=params(16),
+        cost_estimate=cost(0, 4 * rows * width),
+        name="scale_rows",
+    )(plain, vectors)
+
+
+def norm_two(order, inputs, partial, vectors):
+    rows, width = inputs.shape
+    own, from_x, from_y = partial
+
+    def kernel(order_ref, in_ref, own_ref, x_ref, y_ref, vec_ref, mid_ref, out_ref):
+        for place in range(width // LANES):
+            span = slice(place * LANES, (place + 1) * LANES)
+            mid_ref[:, span] = (
+                in_ref[:, lane_block(order_ref[place])]
+                + own_ref[:, span].astype(F32)
+                + x_ref[:, span].astype(F32)
+                + y_ref[:, span].astype(F32)
+            )
+        middle = mid_ref[...]
+        center, inverse = statistics(middle)
+        plain = (middle - center) * inverse
+        out_ref[...] = (plain * vec_ref[2:3, :] + vec_ref[3:4, :]).astype(BF16)
+
+    spec = row_blocks(NORM_ROWS, width)
+    return pl.pallas_call(
+        kernel,
+        grid=(rows // NORM_ROWS,),
+        in_specs=[smem(), spec, spec, spec, spec, whole(8, width)],
+        out_specs=[spec, spec],
+        out_shape=[
+            jax.ShapeDtypeStruct((rows, width), F32),
+            jax.ShapeDtypeStruct((rows, width), BF16),
+        ],
+        compiler_params=params(16),
+        cost_estimate=cost(0, 16 * rows * width),
+        name="norm_two",
+    )(order, inputs, own, from_x, from_y, vectors)
+
+
+def finish_out(order, middle, partial):
+    rows, width = middle.shape
+    own, from_x, from_y = partial
+
+    def kernel(order_ref, mid_ref, own_ref, x_ref, y_ref, out_ref):
+        for place in range(width // LANES):
+            span = slice(place * LANES, (place + 1) * LANES)
+            out_ref[:, lane_block(order_ref[place])] = (
+                mid_ref[:, span]
+                + own_ref[:, span].astype(F32)
+                + x_ref[:, span].astype(F32)
+                + y_ref[:, span].astype(F32)
+            )
+
+    spec = row_blocks(NORM_ROWS, width)
+    return pl.pallas_call(
+        kernel,
+        grid=(rows // NORM_ROWS,),
+        in_specs=[smem(), spec, spec, spec, spec],
+        out_specs=spec,
+        out_shape=jax.ShapeDtypeStruct((rows, width), F32),
+        compiler_params=params(16),
+        cost_estimate=cost(0, 14 * rows * width),
+        name="finish_out",
+    )(order, middle, own, from_x, from_y)
+
+
+def norm_pull(upstream, plain, inverse, gain):
+    scaled = upstream * gain
+    return inverse * (
+        scaled
+        - jnp.mean(scaled, axis=-1, keepdims=True)
+        - plain * jnp.mean(scaled * plain, axis=-1, keepdims=True)
+    )
+
+
+def add_sums(sum_ref, upstream, plain):
+    @pl.when(pl.program_id(0) == 0)
+    def clear():
+        sum_ref[...] = jnp.zeros_like(sum_ref)
+
+    sum_ref[0:1, :] += jnp.sum(upstream * plain, axis=0, keepdims=True)
+    sum_ref[1:2, :] += jnp.sum(upstream, axis=0, keepdims=True)
+
+
+def norm_two_back(order, cotangent, middle, partial, vectors):
+    rows, width = middle.shape
+    own, from_x, from_y = partial
+
+    def kernel(
+        order_ref, cot_ref, mid_ref, own_ref, x_ref, y_ref, vec_ref, grad_ref, low_ref, sum_ref
+    ):
+        middle_rows = mid_ref[...]
+        center, inverse = statistics(middle_rows)
+        plain = (middle_rows - center) * inverse
+        upstream = own_ref[...].astype(F32) + x_ref[...].astype(F32) + y_ref[...].astype(F32)
+        add_sums(sum_ref, upstream, plain)
+        grad_ref[...] = norm_pull(upstream, plain, inverse, vec_ref[2:3, :])
+        for place in range(width // LANES):
+            span = slice(place * LANES, (place + 1) * LANES)
+            total = grad_ref[:, span] + cot_ref[:, lane_block(order_ref[place])]
+            grad_ref[:, span] = total
+            low_ref[:, span] = total.astype(BF16)
+
+    spec = row_blocks(NORM_ROWS, width)
+    return pl.pallas_call(
+        kernel,
+        grid=(rows // NORM_ROWS,),
+        in_specs=[smem(), spec, spec, spec, spec, spec, whole(8, width)],
+        out_specs=[spec, spec, whole(8, width)],
+        out_shape=[
+            jax.ShapeDtypeStruct((rows, width), F32),
+            jax.ShapeDtypeStruct((rows, width), BF16),
+            jax.ShapeDtypeStruct((8, width), F32),
+        ],
+        compiler_params=params(16),
+        cost_estimate=cost(0, 20 * rows * width),
+        name="norm_two_back",
+    )(order, cotangent, middle, own, from_x, from_y, vectors)
+
+
+def norm_one_back(order, inputs, middle_grad, partial, vectors):
+    rows, width = inputs.shape
+    own, from_x, from_y = partial
+
+    def kernel(
+        order_ref,
+        in_ref,
+        mid_ref,
+        own_ref,
+        x_ref,
+        y_ref,
+        vec_ref,
+        out_ref,
+        sum_ref,
+        plain_ref,
+        pull_ref,
+    ):
+        center, inverse = statistics(in_ref[...])
+        for place in range(width // LANES):
+            span = slice(place * LANES, (place + 1) * LANES)
+            plain_ref[:, span] = (in_ref[:, lane_block(order_ref[place])] - center) * inverse
+        plain = plain_ref[...]
+        upstream = own_ref[...].astype(F32) + x_ref[...].astype(F32) + y_ref[...].astype(F32)
+        add_sums(sum_ref, upstream, plain)
+        pull_ref[...] = norm_pull(upstream, plain, inverse, vec_ref[0:1, :])
+        for place in range(width // LANES):
+            span = slice(place * LANES, (place + 1) * LANES)
+            out_ref[:, lane_block(order_ref[place])] = mid_ref[:, span] + pull_ref[:, span]
+
+    spec = row_blocks(NORM_ROWS, width)
+    return pl.pallas_call(
+        kernel,
+        grid=(rows // NORM_ROWS,),
+        in_specs=[smem(), spec, spec, spec, spec, spec, whole(8, width)],
+        out_specs=[spec, whole(8, width)],
+        out_shape=[
+            jax.ShapeDtypeStruct((rows, width), F32),
+            jax.ShapeDtypeStruct((8, width), F32),
+        ],
+        scratch_shapes=[pltpu.VMEM((NORM_ROWS, width), F32), pltpu.VMEM((NORM_ROWS, width), F32)],
+        compiler_params=params(16),
+        cost_estimate=cost(0, 18 * rows * width),
+        name="norm_one_back",
+    )(order, inputs, middle_grad, own, from_x, from_y, vectors)
+
+
+def spread_vectors(sorted_slots, head_slots, gathered):
+    places = sorted_slots.shape[0]
+    heads = head_slots.shape[0]
+
+    def kernel(sorted_ref, head_ref, in_ref, vec_ref, bias_ref):
+        for place in range(places):
+            vec_ref[:, place * LANES : (place + 1) * LANES] = in_ref[sorted_ref[place]].astype(F32)
+        for place in range(heads):
+            bias_ref[:, place * LANES : (place + 1) * LANES] = in_ref[head_ref[place]].astype(F32)
+
+    return pl.pallas_call(
+        kernel,
+        in_specs=[smem(), smem(), pl.BlockSpec(memory_space=pltpu.VMEM)],
+        out_shape=[
+            jax.ShapeDtypeStruct((16, places * LANES), F32),
+            jax.ShapeDtypeStruct((16, heads * LANES), F32),
+        ],
+        compiler_params=params(16),
+        name="spread_vectors",
+    )(sorted_slots, head_slots, gathered)
+
+
+def place_vector_grads(head_places, sums_one, sums_two, bias_sums):
+    heads = head_places.shape[0]
+
+    def kernel(head_ref, one_ref, two_ref, bias_ref, out_ref):
+        out_ref[0:2, :] = one_ref[0:2, :]
+        out_ref[2:4, :] = two_ref[0:2, :]
+        out_ref[4:8, :] = jnp.zeros((4, out_ref.shape[1]), F32)
+        for place in range(heads):
+            for kind in range(3):
+                first = (kind * heads + place) * LANES
+                out_ref[4 + kind : 5 + kind, lane_block(head_ref[place])] = bias_ref[
+                    0:1, first : first + LANES
+                ]
+
+    return pl.pallas_call(
+        kernel,
+        in_specs=[smem()] + [pl.BlockSpec(memory_space=pltpu.VMEM)] * 3,
+        out_shape=jax.ShapeDtypeStruct(sums_one.shape, F32),
+        compiler_params=params(16),
+        name="place_vector_grads",
+    )(head_places, sums_one, sums_two, bias_sums)
+
+
+def adam_vector(keep, home_places, states, gradient, rate):
+    kinds, rows = states[0].shape
+    block = rows // CAP
+
+    def kernel(keep_ref, home_ref, m_ref, f_ref, s_ref, g_ref, mo_ref, fo_ref, so_ref):
+        for slot in range(CAP):
+            span = slice(slot * block, (slot + 1) * block)
+            grad = g_ref[:, lane_block(home_ref[slot])][:kinds]
+            mo_ref[:, span], fo_ref[:, span], so_ref[:, span] = adam_update(
+                m_ref[:, span], f_ref[:, span], s_ref[:, span], grad, keep_ref[slot] > 0, rate
+            )
+
+    return pl.pallas_call(
+        kernel,
+        in_specs=[smem(), smem()] + [pl.BlockSpec(memory_space=pltpu.VMEM)] * 4,
+        out_shape=[jax.ShapeDtypeStruct(states[0].shape, F32)] * 3,
+        compiler_params=params(16),
+        name="adam_vector",
+    )(keep, home_places, *states, gradient)
+
+
+def lane_tables(seq_len):
+    half = ROT // 2
+    frequency = (ROTARY_BASE ** (-2.0 * np.arange(half, dtype=np.float32) / ROT)).astype(np.float32)
+    angles = np.arange(seq_len, dtype=np.float32)[:, None] * frequency[None, :]
+    cosine = np.cos(angles).astype(np.float32)
+    sine = np.sin(angles).astype(np.float32)
+    rest = HEAD_DIM - ROT
+    ones = np.ones((seq_len, rest), np.float32)
+    none = np.zeros((seq_len, rest), np.float32)
+    blank = np.zeros((seq_len, half), np.float32)
+    keep = np.concatenate([cosine, cosine, ones], axis=1)
+    lower = np.concatenate([-sine, blank, none], axis=1)
+    upper = np.concatenate([blank, sine, none], axis=1)
+    return tuple(jnp.asarray(np.concatenate([table, table], axis=1)) for table in (keep, lower, upper))
+
+
+def turn(values, keep, lower, upper):
+    half = ROT // 2
+    return (
+        values * keep
+        + pltpu.roll(values, LANES - half, 1) * lower
+        + pltpu.roll(values, half, 1) * upper
+    )
+
+
+def head_mask(rows, head):
+    lanes = lax.broadcasted_iota(jnp.int32, (rows, LANES), 1)
+    return (lanes // HEAD_DIM) == head
+
+
+def dot_nt(left, right):
+    return lax.dot_general(left, right, (((1,), (1,)), ((), ())), preferred_element_type=F32)
+
+
+def dot_nn(left, right):
+    return lax.dot_general(left, right, (((1,), (0,)), ((), ())), preferred_element_type=F32)
+
+
+def fill_masks(starts_ref, mask_ref, region):
+    for part in range(2):
+        keys = part * region + lax.broadcasted_iota(jnp.int32, (region, region), 0)
+        queries = part * region + lax.broadcasted_iota(jnp.int32, (region, region), 1)
+        visible = keys <= queries
+        for image in range(starts_ref.shape[1]):
+            first = starts_ref[0, image]
+            visible = visible | (
+                (keys >= first)
+                & (keys < first + IMG)
+                & (queries >= first)
+                & (queries < first + IMG)
+            )
+        mask_ref[part] = jnp.where(visible, 0.0, MASKED_SCORE)
+
+
+def tile_scores(key_rows, query_tile, mask_ref, part, first, tile, region):
+    scores = dot_nt(key_rows, query_tile)
+    mask = mask_ref[part, :, first : first + tile]
+    if part == 0:
+        return scores + mask
+    return jnp.concatenate([scores[:region], scores[region:] + mask], axis=0)
+
+
+def attend(row, starts, mixed, bias, tables):
+    seq_len = mixed.shape[0]
+    width = mixed.shape[1] // 3
+    pairs = width // LANES
+    tile = seq_len // 4
+    region = seq_len // 2
+    scale = 1.0 / math.sqrt(HEAD_DIM)
+
+    def kernel(
+        row_ref,
+        starts_ref,
+        q_ref,
+        k_ref,
+        v_ref,
+        qb_ref,
+        kb_ref,
+        vb_ref,
+        keep_ref,
+        lower_ref,
+        upper_ref,
+        out_ref,
+        qo_ref,
+        ko_ref,
+        vo_ref,
+        log_ref,
+        mask_ref,
+    ):
+        @pl.when(pl.program_id(0) == 0)
+        def masks():
+            fill_masks(starts_ref, mask_ref, region)
+
+        for number in range(4):
+            place = slice(number * tile, (number + 1) * tile)
+            origin = pl.ds(pl.multiple_of(jnp.bitwise_xor(row_ref[0], number) * tile, tile), tile)
+            turns = (keep_ref[place, :], lower_ref[place, :], upper_ref[place, :])
+            turned = turn(q_ref[origin, :] + qb_ref[4:5, :], *turns)
+            qo_ref[place, :] = (turned.astype(BF16).astype(F32) * scale).astype(BF16)
+            ko_ref[place, :] = turn(k_ref[origin, :] + kb_ref[5:6, :], *turns).astype(BF16)
+            vo_ref[place, :] = (v_ref[origin, :] + vb_ref[6:7, :]).astype(BF16)
+        value_columns = jnp.transpose(vo_ref[...])
+        for number in range(4):
+            part = number // 2
+            seen = region * (part + 1)
+            first = (number % 2) * tile
+            outs = []
+            for head in range(2):
+                query_tile = jnp.where(
+                    head_mask(tile, head),
+                    qo_ref[number * tile : (number + 1) * tile, :],
+                    jnp.zeros((), BF16),
+                )
+                scores = tile_scores(
+                    ko_ref[:seen, :], query_tile, mask_ref, part, first, tile, region
+                )
+                peak = jnp.max(scores, axis=0, keepdims=True)
+                powers = jnp.exp(scores - peak)
+                total = jnp.sum(powers, axis=0, keepdims=True)
+                log_ref[0, head : head + 1, number * tile : (number + 1) * tile] = peak + jnp.log(
+                    total
+                )
+                mixed_values = dot_nn(
+                    value_columns[head * HEAD_DIM : (head + 1) * HEAD_DIM, :seen],
+                    powers.astype(BF16),
+                )
+                outs.append(mixed_values / total)
+            place = pl.ds(pl.multiple_of(jnp.bitwise_xor(row_ref[0], number) * tile, tile), tile)
+            out_ref[place, :] = jnp.transpose(jnp.concatenate(outs, axis=0)).astype(BF16)
+
+    def columns(kind):
+        return pl.BlockSpec((seq_len, LANES), lambda h: (0, kind * pairs + h))
+
+    bias_block = pl.BlockSpec((8, LANES), lambda h: (0, h))
+    table = pl.BlockSpec((seq_len, LANES), lambda h: (0, 0))
+    low = jax.ShapeDtypeStruct((seq_len, width), BF16)
+    return pl.pallas_call(
+        kernel,
+        grid=(pairs,),
+        in_specs=[smem(), smem()]
+        + [columns(0), columns(1), columns(2)]
+        + [bias_block] * 3
+        + [table] * 3,
+        out_specs=[columns(0)] * 4 + [pl.BlockSpec((1, 8, seq_len), lambda h: (h, 0, 0))],
+        out_shape=[low] * 4 + [jax.ShapeDtypeStruct((pairs, 8, seq_len), F32)],
+        scratch_shapes=[pltpu.VMEM((2, region, region), F32)],
+        compiler_params=params(40),
+        cost_estimate=cost(
+            3 * seq_len * seq_len * width * 4, 20 * seq_len * width, seq_len * seq_len * 2 * pairs
+        ),
+        name="attend",
+    )(row, starts, mixed, mixed, mixed, bias, bias, bias, *tables)
+
+
+def attend_back(row, starts, queries, keys, values, logs, outputs, grads, tables):
+    seq_len, width = queries.shape
+    pairs = width // LANES
+    tile = seq_len // 4
+    region = seq_len // 2
+    scale = 1.0 / math.sqrt(HEAD_DIM)
+
+    def kernel(
+        row_ref,
+        starts_ref,
+        q_ref,
+        k_ref,
+        v_ref,
+        log_ref,
+        o_ref,
+        g_ref,
+        keep_ref,
+        lower_ref,
+        upper_ref,
+        out_ref,
+        sum_ref,
+        mask_ref,
+        dq_ref,
+        dk_ref,
+        dv_ref,
+        low_ref,
+        bias_ref,
+    ):
+        @pl.when((pl.program_id(0) == 0) & (pl.program_id(1) == 0))
+        def masks():
+            fill_masks(starts_ref, mask_ref, region)
+
+        @pl.when(pl.program_id(1) == 0)
+        def work():
+            dk_ref[...] = jnp.zeros_like(dk_ref)
+            dv_ref[...] = jnp.zeros_like(dv_ref)
+            key_columns = jnp.transpose(k_ref[...])
+            for number in range(4):
+                part = number // 2
+                seen = region * (part + 1)
+                first = (number % 2) * tile
+                span = slice(number * tile, (number + 1) * tile)
+                origin = pl.ds(
+                    pl.multiple_of(jnp.bitwise_xor(row_ref[0], number) * tile, tile), tile
+                )
+                grad_tile = g_ref[origin, :]
+                products = jnp.transpose(grad_tile.astype(F32) * o_ref[origin, :].astype(F32))
+                query_grads = []
+                for head in range(2):
+                    mine = head_mask(tile, head)
+                    query_tile = jnp.where(mine, q_ref[span, :], jnp.zeros((), BF16))
+                    head_grad = jnp.where(mine, grad_tile, jnp.zeros((), BF16))
+                    inner = jnp.sum(
+                        products[head * HEAD_DIM : (head + 1) * HEAD_DIM], axis=0, keepdims=True
+                    )
+                    scores = tile_scores(
+                        k_ref[:seen, :], query_tile, mask_ref, part, first, tile, region
+                    )
+                    weights = jnp.exp(scores - log_ref[0, head : head + 1, span])
+                    pulls = dot_nt(v_ref[:seen, :], head_grad)
+                    score_grad = (weights * (pulls - inner)).astype(BF16)
+                    dv_ref[:seen, :] += dot_nn(weights.astype(BF16), head_grad)
+                    dk_ref[:seen, :] += dot_nn(score_grad, query_tile)
+                    query_grads.append(
+                        dot_nn(
+                            key_columns[head * HEAD_DIM : (head + 1) * HEAD_DIM, :seen], score_grad
+                        )
+                    )
+                dq_ref[span, :] = jnp.transpose(jnp.concatenate(query_grads, axis=0)) * scale
+            bias_ref[...] = jnp.zeros_like(bias_ref)
+            for number in range(4):
+                span = slice(number * tile, (number + 1) * tile)
+                origin = pl.ds(
+                    pl.multiple_of(jnp.bitwise_xor(row_ref[0], number) * tile, tile), tile
+                )
+                turns = (keep_ref[span, :], -lower_ref[span, :], -upper_ref[span, :])
+                parts = (
+                    turn(dq_ref[span, :], *turns),
+                    turn(dk_ref[span, :], *turns),
+                    dv_ref[span, :],
+                )
+                for kind in range(3):
+                    low = parts[kind].astype(BF16)
+                    low_ref[kind, origin, :] = low
+                    bias_ref[kind, 0:1, :] += jnp.sum(low.astype(F32), axis=0, keepdims=True)
+
+        out_ref[...] = low_ref[pl.program_id(1)]
+        sum_ref[...] = bias_ref[pl.program_id(1)]
+
+    columns = pl.BlockSpec((seq_len, LANES), lambda h, j: (0, h))
+    table = pl.BlockSpec((seq_len, LANES), lambda h, j: (0, 0))
+    return pl.pallas_call(
+        kernel,
+        grid=(pairs, 3),
+        in_specs=[smem(), smem()]
+        + [columns] * 3
+        + [pl.BlockSpec((1, 8, seq_len), lambda h, j: (h, 0, 0))]
+        + [columns] * 2
+        + [table] * 3,
+        out_specs=[
+            pl.BlockSpec((seq_len, LANES), lambda h, j: (0, j * pairs + h)),
+            pl.BlockSpec((8, LANES), lambda h, j: (0, j * pairs + h)),
+        ],
+        out_shape=[
+            jax.ShapeDtypeStruct((seq_len, 3 * width), BF16),
+            jax.ShapeDtypeStruct((8, 3 * width), F32),
+        ],
+        scratch_shapes=[
+            pltpu.VMEM((2, region, region), F32),
+            pltpu.VMEM((seq_len, LANES), F32),
+            pltpu.VMEM((seq_len, LANES), F32),
+            pltpu.VMEM((seq_len, LANES), F32),
+            pltpu.VMEM((3, seq_len, LANES), BF16),
+            pltpu.VMEM((3, 8, LANES), F32),
+        ],
+        compiler_params=params(48),
+        cost_estimate=cost(
+            8 * seq_len * seq_len * width * 4, 20 * seq_len * width, seq_len * seq_len * 2 * pairs
+        ),
+        name="attend_back",
+    )(row, starts, queries, keys, values, logs, outputs, grads, *tables)
+
+
+def gate_up(rows_two, w_gate):
+    tokens, width = rows_two.shape
+    tiles = w_gate.shape[1] // (2 * LANES)
+
+    def kernel(in_ref, w_ref, gate_ref, up_ref, hidden_ref):
+        both = dot_nn(in_ref[...], w_ref[...])
+        gate, up = both[:, :LANES], both[:, LANES:]
+        gate_ref[...] = gate.astype(BF16)
+        up_ref[...] = up.astype(BF16)
+        hidden_ref[...] = (gate * jax.nn.sigmoid(gate) * up).astype(BF16)
+
+    out = pl.BlockSpec((tokens, LANES), lambda i: (0, i))
+    return pl.pallas_call(
+        kernel,
+        grid=(tiles,),
+        in_specs=[whole(tokens, width), pl.BlockSpec((width, 2 * LANES), lambda i: (0, i))],
+        out_specs=[out] * 3,
+        out_shape=[jax.ShapeDtypeStruct((tokens, tiles * LANES), BF16)] * 3,
+        compiler_params=params(40),
+        cost_estimate=cost(
+            2 * tokens * w_gate.size,
+            2 * (rows_two.size + w_gate.size) + 6 * tokens * tiles * LANES,
+            tokens * tiles * LANES,
+        ),
+        name="gate_up",
+    )(rows_two, w_gate)
+
+
+def gate_up_back(rows_grad, w_down, gate, up):
+    tokens, width = rows_grad.shape
+    hidden = w_down.shape[1]
+    tile = 256
+
+    def kernel(in_ref, w_ref, gate_ref, up_ref, out_ref):
+        pulled = dot_nn(in_ref[...], w_ref[...])
+        for number in range(hidden // LANES):
+            span = slice(number * LANES, (number + 1) * LANES)
+            grad = pulled[:, span]
+            gate_part = gate_ref[:, span].astype(F32)
+            up_part = up_ref[:, span].astype(F32)
+            squash = jax.nn.sigmoid(gate_part)
+            first = 2 * number * LANES
+            out_ref[:, first : first + LANES] = (
+                grad * up_part * squash * (1.0 + gate_part * (1.0 - squash))
+            ).astype(BF16)
+            out_ref[:, first + LANES : first + 2 * LANES] = (grad * gate_part * squash).astype(BF16)
+
+    return pl.pallas_call(
+        kernel,
+        grid=(tokens // tile,),
+        in_specs=[
+            row_blocks(tile, width),
+            whole(width, hidden),
+            row_blocks(tile, hidden),
+            row_blocks(tile, hidden),
+        ],
+        out_specs=row_blocks(tile, 2 * hidden),
+        out_shape=jax.ShapeDtypeStruct((tokens, 2 * hidden), BF16),
+        compiler_params=params(40),
+        cost_estimate=cost(
+            2 * tokens * w_down.size,
+            2 * (rows_grad.size + w_down.size) + 8 * tokens * hidden,
+            tokens * hidden,
+        ),
+        name="gate_up_back",
+    )(rows_grad, w_down, gate, up)
+
+
+def adam_update(master, first, second, gradient, keep, rate):
+    correction = 1.0 - MOMENT_DECAY**STEP
+    new_first = MOMENT_DECAY * first + (1.0 - MOMENT_DECAY) * gradient
+    new_second = MOMENT_DECAY * second + (1.0 - MOMENT_DECAY) * gradient * gradient
+    direction = new_first / correction / (jnp.sqrt(new_second / correction) + ADAM_EPSILON)
+    new_master = master - rate * (direction + WEIGHT_DECAY * master)
+    return (
+        jnp.where(keep, new_master, master),
+        jnp.where(keep, new_first, first),
+        jnp.where(keep, new_second, second),
+    )
+
+
+def adam_call(name, keep, states, gradient, rate, grid, state_spec, grad_spec, pieces):
+    def kernel(keep_ref, m_ref, f_ref, s_ref, g_ref, mo_ref, fo_ref, so_ref):
+        live = keep_ref[pl.program_id(0)] > 0
+        for state_at, grad_at in pieces:
+            results = adam_update(
+                m_ref[state_at],
+                f_ref[state_at],
+                s_ref[state_at],
+                g_ref[grad_at].astype(F32),
+                live,
+                rate,
+            )
+            mo_ref[state_at], fo_ref[state_at], so_ref[state_at] = results
+
+    return pl.pallas_call(
+        kernel,
+        grid=grid,
+        in_specs=[smem()] + [state_spec] * 3 + [grad_spec],
+        out_specs=[state_spec] * 3,
+        out_shape=[jax.ShapeDtypeStruct(states[0].shape, F32)] * 3,
+        compiler_params=params(40),
+        cost_estimate=cost(12 * states[0].size, 26 * states[0].size, states[0].size),
+        name=name,
+    )(keep, *states, gradient)
+
+
+def adam_query(keep, states, gradient, rate):
+    kinds, rows, width = states[0].shape
+    block = rows // CAP
+    return adam_call(
+        "adam_query",
+        keep,
+        states,
+        gradient,
+        rate,
+        (CAP, kinds),
+        pl.BlockSpec((1, block, width), lambda s, j: (j, s, 0)),
+        pl.BlockSpec((1, block, width), lambda s, j: (s, 0, j)),
+        [((0,), (0,))],
+    )
+
+
+def adam_flat(name, keep, states, gradient, rate):
+    rows, width = states[0].shape
+    block = rows // CAP
+    return adam_call(
+        name,
+        keep,
+        states,
+        gradient,
+        rate,
+        (CAP,),
+        pl.BlockSpec((block, width), lambda s: (s, 0)),
+        pl.BlockSpec((1, block, width), lambda s: (s, 0, 0)),
+        [((slice(None), slice(None)), (0,))],
+    )
+
+
+def adam_gate(keep, states, gradient, rate):
+    block, width = gradient.shape[1:]
+    tiles = width // LANES
+    part = block // 2
+    pieces = [
+        (
+            (pl.ds(tile, part, stride=tiles), slice(None)),
+            (0, slice(None), slice(tile * LANES, (tile + 1) * LANES)),
+        )
+        for tile in range(tiles)
+    ]
+    return adam_call(
+        "adam_gate",
+        keep,
+        states,
+        gradient,
+        rate,
+        (CAP, 2),
+        pl.BlockSpec((part * tiles, LANES), lambda s, i: (2 * s + i, 0)),
+        pl.BlockSpec((1, part, width), lambda s, i: (s, i, 0)),
+        pieces,
+    )
+
+
+def matmul(left, right, left_dim, right_dim, dtype):
+    return lax.dot_general(
+        left, right, (((left_dim,), (right_dim,)), ((), ())), preferred_element_type=F32
+    ).astype(dtype)
+
+
+def flips(axis, reach):
+    return [(index, index ^ reach) for index in range(lax.axis_size(axis))]
+
+
+def x_pairs():
+    return flips("row", 1)
+
+
+def y_pairs():
+    return flips("row", 2)
+
+
+def share_rows(own):
+    half = own.shape[0] // 2
+    by_x = lax.ppermute(own, "row", x_pairs())
+    by_y = lax.ppermute(own, "row", y_pairs())
+    top = lax.ppermute(by_x[:half], "row", y_pairs())
+    bottom = lax.ppermute(by_y[half:], "row", x_pairs())
+    return jnp.concatenate([own, by_x, by_y, top, bottom], axis=0), by_x, by_y
+
+
+def scatter_rows(sums):
+    rows = sums.shape[0] // 4
+    half = rows // 2
+    top = lax.ppermute(sums[3 * rows : 3 * rows + half], "row", y_pairs())
+    bottom = lax.ppermute(sums[3 * rows + half :], "row", x_pairs())
+    to_x = jnp.concatenate([sums[rows : rows + half] + top, sums[rows + half : 2 * rows]], axis=0)
+    to_y = jnp.concatenate(
+        [sums[2 * rows : 2 * rows + half], sums[2 * rows + half : 3 * rows] + bottom], axis=0
+    )
+    return (
+        (sums, lax.ppermute(to_x, "row", x_pairs()), lax.ppermute(to_y, "row", y_pairs())),
+        to_x,
+        to_y,
+    )
+
+
+def chip_moves(columns, moves):
+    chips = columns // 2
+    return [
+        (2 * chip + core, 2 * (chip + moves[core]) + core)
+        for chip in range(chips)
+        for core in range(2)
+        if 0 <= chip + moves[core] < chips
+    ]
+
+
+def swap_cores(values, columns):
+    return lax.ppermute(values, "col", [(index, index ^ 1) for index in range(columns)])
+
+
+def both_cores(values, columns):
+    return values, swap_cores(values, columns)
+
+
+def local_line(
+    inputs,
+    cotangent,
+    image_starts,
+    owners,
+    query_master,
+    query_first,
+    query_second,
+    output_master,
+    output_first,
+    output_second,
+    gate_master,
+    gate_first,
+    gate_second,
+    down_master,
+    down_first,
+    down_second,
+    vector_master,
+    vector_first,
+    vector_second,
+):
+    columns = lax.axis_size("col")
+    col_index = lax.axis_index("col")
+    row_index = lax.axis_index("row")
+    blocks = owners.shape[0]
+    block_rows = D // blocks
+    chip, core = col_index // 2, col_index % 2
+
+    slot_of = owner_slots(owners)
+    numbers = jnp.arange(blocks, dtype=jnp.int32)
+    place_of = jnp.sum((slot_of[None, :] < slot_of[:, None]).astype(jnp.int32), axis=1)
+    at_place = place_of[None, :] == numbers[:, None]
+    order = jnp.sum(jnp.where(at_place, numbers[None, :], 0), axis=1)
+    sorted_slots = jnp.sum(jnp.where(at_place, slot_of[None, :], 0), axis=1)
+    head_blocks = query_master.shape[2] // LANES
+    head_slots = lax.dynamic_slice_in_dim(slot_of, row_index * head_blocks, head_blocks, 0)
+    head_places = lax.dynamic_slice_in_dim(place_of, row_index * head_blocks, head_blocks, 0)
+
+    def owned_below(index):
+        return jnp.sum((owners < index).astype(jnp.int32))
+
+    chip_first = owned_below(2 * chip)
+    chip_middle = owned_below(2 * chip + 1)
+    chip_end = owned_below(2 * chip + 2)
+    own_first = owned_below(col_index)
+    own_count = owned_below(col_index + 1) - own_first
+    chip_numbers = jnp.arange(columns // 2, dtype=jnp.int32)
+    below = jnp.sum((owners[None, :] < 2 * chip_numbers[:, None]).astype(jnp.int32), axis=1)
+    uneven = jnp.max(jnp.abs(below - 4 * chip_numbers)) > 2
+
+    def chip_code(place):
+        owner_core = (place >= chip_middle).astype(jnp.int32)
+        rank = place - jnp.where(owner_core > 0, chip_middle, chip_first)
+        code = jnp.where(owner_core == core, 0, 16) + rank
+        return jnp.where((place >= chip_first) & (place < chip_end), code, 0)
+
+    pair = jnp.arange(2, dtype=jnp.int32)
+    toward = jnp.where(core == 0, 1, -1)
+    kept_place = 4 * chip + 2 * core + pair
+    near_code = 32 + pair
+    far_code = 48 + pair
+    keep_codes = jnp.where(
+        kept_place < chip_first,
+        jnp.where(core == 0, near_code, far_code),
+        jnp.where(
+            kept_place >= chip_end,
+            jnp.where(core == 0, far_code, near_code),
+            chip_code(kept_place),
+        ),
+    )
+    four = jnp.arange(CAP, dtype=jnp.int32)
+    live = (four < own_count).astype(jnp.int32)
+    home_places = own_first + jnp.minimum(four, own_count - 1)
+    home_side = home_places // 4 - chip
+    home_core = (home_places % 4) // 2
+    near_side = jnp.where(home_core == 0, 1, -1)
+    home_source = jnp.where(home_side == 0, 0, jnp.where(home_side == near_side, 1, 4))
+    home_other = jnp.where(home_source == 4, 5, home_source + 2)
+    codes = jnp.concatenate(
+        [
+            chip_code(4 * (chip + toward) + 2 * core + pair),
+            chip_code(4 * (chip - toward) + 2 * core + pair),
+            keep_codes,
+            16 * jnp.where(home_core == core, home_source, home_other) + home_places % 2,
+        ]
+    )
+
+    inward = chip_moves(columns, (1, -1))
+    outward = chip_moves(columns, (-1, 1))
+
+    def spread_out(own, send_codes, keep_codes):
+        partner = swap_cores(own, columns)
+        sent = pick_blocks(send_codes, 0, 2, [own, partner])
+        near = lax.ppermute(sent, "col", inward)
+
+        def farther():
+            far = lax.ppermute(pick_blocks(codes, 2, 2, [own, partner]), "col", outward)
+            return pick_blocks(keep_codes, 4, 2, [own, partner, near, far])
+
+        kept = lax.cond(
+            uneven, farther, lambda: pick_blocks(keep_codes, 4, 2, [own, partner, near])
+        )
+        return sent, kept.reshape(2 * block_rows, own.shape[2])
+
+    def gather(part):
+        return lax.all_gather(part, "col", axis=0, tiled=True)
+
+    def sum_up(gradient):
+        own = lax.psum_scatter(gradient, "col", scatter_dimension=0, tiled=True)
+        return own.reshape(2, block_rows, own.shape[1])
+
+    def send_home(own):
+        near = lax.ppermute(own, "col", outward)
+        held = [own, near, swap_cores(own, columns), swap_cores(near, columns)]
+
+        def farther():
+            far = lax.ppermute(own, "col", inward)
+            return pick_blocks(codes, 6, CAP, held + [far, swap_cores(far, columns)])
+
+        return lax.cond(uneven, farther, lambda: pick_blocks(codes, 6, CAP, held))
+
+    local_in = inputs[0]
+    upstream = cotangent[0]
+    row = row_index.reshape(1)
+    tables = lane_tables(inputs.shape[1] * 4)
+    rates = step_rates()
+
+    query_slabs = [
+        jnp.transpose(part, (1, 0, 2)) for part in (query_master, query_first, query_second)
+    ]
+    plain_one = norm_one(order, local_in)
+    rows_plain, *plain_parts = share_rows(plain_one)
+    sent_query, query_part = spread_out(
+        pack_query(query_slabs[0]), after(codes, plain_one), after(codes, *plain_parts)
+    )
+    w_query = gather(query_part)
+    vector_rows = jnp.pad(vector_master.T, ((0, 9), (0, 0))).astype(BF16)
+    vector_blocks = jnp.transpose(vector_rows.reshape(16, CAP, block_rows), (1, 0, 2))
+    vectors, bias = spread_vectors(
+        sorted_slots, head_slots, gather(after(vector_blocks, query_part))
+    )
+    unused, output_part = spread_out(
+        pack_flat("pack_output", output_master),
+        after(codes, rows_plain, vectors),
+        after(codes, query_part),
+    )
+    w_output = gather(output_part)
+    rows_grad = share_rows(order_grad(after(order, rows_plain), upstream))[0]
+    rows_one = scale_rows(rows_plain, vectors)
+    mixed = matmul(rows_one, w_query, 1, 0, F32)
+    gate_states = [gate_lines(part) for part in (gate_master, gate_first, gate_second)]
+    unused, gate_part = spread_out(
+        pack_gate(gate_states[0], gate_master.shape[0]),
+        after(codes, rows_one, output_part),
+        after(codes, mixed),
+    )
+    w_gate = gather(gate_part)
+    attended, queries, keys, values, logs = attend(
+        after(row, gate_part), image_starts, mixed, bias, tables
+    )
+    unused, down_part = spread_out(
+        pack_flat("pack_down", down_master), after(codes, gate_part), after(codes, attended)
+    )
+    w_down = gather(down_part)
+    middle, normed_two = norm_two(
+        order,
+        local_in,
+        scatter_rows(matmul(attended, w_output, 1, 1, BF16))[0],
+        after(vectors, down_part, rows_grad),
+    )
+    rows_two = share_rows(normed_two)[0]
+    gate, up, hidden = gate_up(rows_two, w_gate)
+
+    down_sums = matmul(rows_grad, hidden, 0, 0, BF16)
+    down_own = sum_up(down_sums)
+    gate_up_grad = gate_up_back(rows_grad, w_down, after(gate, down_sums), up)
+    pulled_two = matmul(gate_up_grad, w_gate, 1, 1, BF16)
+    gate_sums = matmul(rows_two, after(gate_up_grad, pulled_two), 0, 0, BF16)
+    gate_own = sum_up(gate_sums)
+    out_sums = matmul(after(hidden, gate_sums), w_down, 1, 1, BF16)
+    middle_grad, low_middle, sums_two = norm_two_back(
+        order, upstream, middle, scatter_rows(pulled_two)[0], after(vectors, gate_sums, out_sums)
+    )
+    rows_mid = share_rows(low_middle)[0]
+    new_down = adam_flat(
+        "adam_down",
+        live,
+        (down_master, down_first, down_second),
+        send_home(after(down_own, low_middle)),
+        rates[3],
+    )
+    attended_grad = matmul(after(rows_mid, new_down[0]), w_output, 1, 0, BF16)
+    output_sums = matmul(rows_mid, after(attended, attended_grad), 0, 0, BF16)
+    output_own = sum_up(output_sums)
+    out_partial, *out_parts = scatter_rows(after(out_sums, attended_grad))
+    mixed_grad, bias_sums = attend_back(
+        after(row, output_sums, *out_parts),
+        image_starts,
+        queries,
+        keys,
+        values,
+        logs,
+        attended,
+        attended_grad,
+        tables,
+    )
+    layer_out = finish_out(order, middle, out_partial)
+    pulled_one = matmul(after(mixed_grad, layer_out), w_query, 1, 1, BF16)
+    query_sums = matmul(rows_one, after(mixed_grad, pulled_one), 0, 0, BF16)
+    query_own = sum_up(query_sums)
+    input_grad, sums_one = norm_one_back(
+        order,
+        local_in,
+        middle_grad,
+        scatter_rows(pulled_one)[0],
+        after(vectors, query_sums),
+    )
+    new_gate = [
+        gate_unlines(part, gate_master.shape)
+        for part in adam_gate(
+            live, gate_states, send_home(after(gate_own, query_sums)), rates[2]
+        )
+    ]
+    vector_sums = place_vector_grads(
+        after(head_places, new_gate[0]), sums_one, sums_two, bias_sums
+    )
+    for axis, reach in (("row", 1), ("row", 2), ("col", 1), ("col", 2), ("col", 4)):
+        vector_sums = vector_sums + lax.ppermute(vector_sums, axis, flips(axis, reach))
+    new_output = adam_flat(
+        "adam_output",
+        live,
+        (output_master, output_first, output_second),
+        send_home(after(output_own, new_gate[0])),
+        rates[1],
+    )
+    new_vector = [
+        part.T
+        for part in adam_vector(
+            live,
+            home_places,
+            [part.T for part in (vector_master, vector_first, vector_second)],
+            vector_sums,
+            rates[4],
+        )
+    ]
+    query_own = after(query_own, new_output[0], new_vector[0], input_grad)
+    new_query = [
+        jnp.transpose(part, (1, 0, 2))
+        for part in adam_query(live, query_slabs, send_home(query_own), rates[0])
+    ]
+    return (
+        layer_out[None],
+        input_grad[None],
+        *new_query,
+        *new_output,
+        *new_gate,
+        *new_down,
+        *new_vector,
+    )
+
+
 def solution(mesh):
+    one_hop_line = mesh.shape["row"] == 4 and mesh.shape["col"] == 8
     return jax.shard_map(
-        local,
+        local_line if one_hop_line else local,
         mesh=mesh,
         in_specs=(
             P("col", "row", None),

time: 1890 us -> 737 us (0.39)
  waiting for transfers between devices: 1210 us -> 255 us
  other arithmetic: 187 us -> 16.6 us
  Pallas kernels: 0 us -> 165 us
  matrix products: 216 us -> 96 us
  local copies, waits for them, and re-layouts: 178 us -> 80.7 us
  starting transfers between devices: 0.54 us -> 82.2 us
  blocking collectives: 59.5 us -> 14.7 us
    all_gather x8 -> x4, waiting for transfers between devices: 564 us -> 0.02 us  [gather(): return lax.all_gather(part, 'col', axis=0, tiled=True)]
    psum x1 -> x0, waiting for transfers between devices: 451 us -> none  [local(): lax.psum(query_weight_grad.astype(jnp.bfloat16), 'col').astype(jnp.float32)]
    ppermute x0 -> x57, waiting for transfers between devices: none -> 255 us  [the longest x4 61.9 us: send_home(): near = lax.ppermute(own, 'col', outward)]
    reduce_scatter x4, waiting for transfers between devices: 199 us -> 0.03 us  [sum_up(): own = lax.psum_scatter(gradient, 'col', scatter_dimension=0, tiled=True)]
    pallas_call x0 -> x34, Pallas kernels: none -> 165 us  [the longest x4 33.3 us: adam_call(): pl.pallas_call(kernel, grid=grid, in_specs=[smem()] + [state_spec] * 3 +...]
    dot_general x26 -> x10, matrix products: 216 us -> 96 us  [matmul(): lax.dot_general(left, right, (((left_dim,), (right_dim,)), ((), ())), pre...]
    gather x14 -> x0, local copies, waits for them, and re-layouts: 101 us -> none  [the longest x7 64.5 us: unpack(): return jnp.take(shaped, slot_of, axis=0).reshape((-1,) + gathered.shape[1:])]
    ppermute x0 -> x57, starting transfers between devices: none -> 81.3 us  [the longest x4 20.3 us: spread_out(): near = lax.ppermute(sent, 'col', inward)]
  transfers between devices with their start and end apart: 13 -> 65, of which waited for: 12 -> 35; matrix products, arithmetic and copies ran while one was open for 11% -> 19% of each run, Pallas kernels for 0% -> 20%
where the time goes in v1:
time: 737 us; the launch traced here: 728 us
  waiting for transfers between devices  255 us (35%)
  Pallas kernels  165 us (22%)
  matrix products  96 us (13%)
  starting transfers between devices  82.2 us (11%)
  local copies, waits for them, and re-layouts  80.7 us (11%)
  between operations  17.5 us (2%)
  other arithmetic  16.6 us (2%)
  blocking collectives  14.7 us (2%)
    dot_general x10, matrix products, matmul(): lax.dot_general(left, right, (((left_dim,), (right_dim,)), ((), ())), pre...  96 us
    unnamed x168, local copies, waits for them, and re-layouts  69.1 us
    ppermute x4, waiting for transfers between devices, send_home(): near = lax.ppermute(own, 'col', outward)  61.9 us
    ppermute x4, waiting for transfers between devices, share_rows(): by_x = lax.ppermute(own, 'row', x_pairs())  54.6 us
    pallas_call x4, Pallas kernels, adam_call(): pl.pallas_call(kernel, grid=grid, in_specs=[smem()] + [state_spec] * 3 +...  33.3 us
    ppermute x4, waiting for transfers between devices, spread_out(): near = lax.ppermute(sent, 'col', inward)  30.1 us
    pallas_call x12, Pallas kernels, pick_blocks(): pl.pallas_call(kernel, in_specs=[smem()] + [pl.BlockSpec(memory_space=pl....  27.3 us
    pallas_call x1, Pallas kernels, attend_back(): pl.pallas_call(kernel, grid=(pairs, 3), in_specs=[smem(), smem()] + [colu...  26.8 us
  transfers between devices with their start and end apart: 65, of which 35 were waited for; matrix products, arithmetic and copies ran while one was open for 19% of the time, Pallas kernels for 20%

profile of v1, /device:TPU:0, one launch (start us, length us, event | category | flops | bytes accessed | tf_op | source)
XLA Modules:
  0.0 728.3 jit_solution(10502745466422278522)
XLA Ops:
  32.7 8.0 %collective-permute-done.13 = bf16[256,2048]{1,0:T(8,128)(2,1)} collective-permute-done((bf16[256,2048]{1,0:T(8,128)(2,1)S(1)}, bf16[256,2048]{1,0:T(8,128)(2,1)}, u32[]{:S(2)}, u32[]{:S(2)}) %collective-permute-start.13) | collective-permute-done | bytes 1048608 | tf_op jit(solution)/shard_map/ppermute | solution.py:1297
  62.9 6.1 collective-permute-done.14
  71.0 14.7 %all_gather.15.in_ref = bf16[32,16,128]{2,1,0:T(8,128)(2,1)S(1)} all-gather(bf16[4,16,128]{2,1,0:T(8,128)(2,1)S(1)} %bitcast_bitcast_fusion), channel_id=1, replica_groups=mesh['row'=4,'col'=8] {'col'}, dimensions={0}, use_global_device_ids=true | all-gather | bytes 147456 | tf_op jit(solution)/shard_map/all_gather | solution.py:1442
  92.1 9.4 %collective-permute-done.20 = bf16[2,128,512]{2,1,0:T(8,128)(2,1)S(1)} collective-permute-done((bf16[2,128,512]{2,1,0:T(8,128)(2,1)S(1)}, bf16[2,128,512]{2,1,0:T(8,128)(2,1)S(1)}, u32[]{:S(2)}, u32[]{:S(2)}) %collective-permute-start.20) | collective-permute-done | bytes 262176 | tf_op jit(solution)/shard_map/ppermute | solution.py:1430
  112.1 7.3 %collective-permute-start.21 = (bf16[2,128,2816]{2,1,0:T(8,128)(2,1)}, bf16[2,128,2816]{2,1,0:T(8,128)(2,1)}, u32[]{:S(2)}, u32[]{:S(2)}) collective-permute-start(bf16[2,128,2816]{2,1,0:T(8,128)(2,1)} %pick_blocks.46), channel_id=1, source_target_pairs={{0,2},{2,4},{3,1},{4,6},{5,3},{7,5},{8,10},{10,12},{11,9},{12,14},... | collective-permute-start | bytes 4325384 | tf_op jit(solution)/shard_map/ppermute | solution.py:1430
  119.5 11.9 %fusion.17.q_ref.k_ref.v_ref = f32[1024,1536]{1,0:T(8,128)} fusion(bf16[1024,2048]{1,0:T(8,128)(2,1)} %copy-done.18, bf16[2048,1536]{1,0:T(8,128)(2,1)} %all-gather.5.cloned.1.call-done), kind=kOutput, calls=%fused_computation.115 | convolution fusion | flops 6442450944 | bytes 16777216 | tf_op jit(solution)/shard_map/dot_general | solution.py:1277
  131.4 20.7 %collective-permute-done.21 = bf16[2,128,2816]{2,1,0:T(8,128)(2,1)} collective-permute-done((bf16[2,128,2816]{2,1,0:T(8,128)(2,1)}, bf16[2,128,2816]{2,1,0:T(8,128)(2,1)}, u32[]{:S(2)}, u32[]{:S(2)}) %collective-permute-start.21) | collective-permute-done | bytes 1441824 | tf_op jit(solution)/shard_map/ppermute | solution.py:1430
  167.0 22.9 %attend.1 = (bf16[1024,512]{1,0:T(8,128)(2,1)S(1)}, bf16[1024,512]{1,0:T(8,128)(2,1)S(1)}, bf16[1024,512]{1,0:T(8,128)(2,1)S(1)}, bf16[1024,512]{1,0:T(8,128)(2,1)S(1)}, f32[4,8,1024]{2,1,0:T(8,128)S(1)}) custom-call(s32[1]{0:T(128)} %bitcast.9.row_ref, s32[1,2]{1,0:T(1,128)S(1)} %copy-done.40, f32[1024,1536]{1,0:T(8,128)S(1)} %copy-done.51, ...), custom_call_target="tpu_custom_call" | custom-call | flops 6442450944 | bytes 10485760 | tf_op jit(solution)/shard_map/attend/pallas_call | solution.py:972
  207.1 17.6 %collective-permute-done.28 = bf16[256,2048]{1,0:T(8,128)(2,1)} collective-permute-done((bf16[256,2048]{1,0:T(8,128)(2,1)S(1)}, bf16[256,2048]{1,0:T(8,128)(2,1)}, u32[]{:S(2)}, u32[]{:S(2)}) %collective-permute-start.28) | collective-permute-done | bytes 1048608 | tf_op jit(solution)/shard_map/ppermute | solution.py:1296
  245.7 8.0 %collective-permute-done.30 = bf16[128,2048]{1,0:T(8,128)(2,1)S(1)} collective-permute-done((bf16[128,2048]{1,0:T(8,128)(2,1)S(1)}, bf16[128,2048]{1,0:T(8,128)(2,1)S(1)}, u32[]{:S(2)}, u32[]{:S(2)}) %collective-permute-start.30) | collective-permute-done | bytes 524320 | tf_op jit(solution)/shard_map/ppermute | solution.py:1298
  253.7 12.6 %collective-permute-done.31 = bf16[128,2048]{1,0:T(8,128)(2,1)S(1)} collective-permute-done((bf16[128,2048]{1,0:T(8,128)(2,1)S(1)}, bf16[128,2048]{1,0:T(8,128)(2,1)S(1)}, u32[]{:S(2)}, u32[]{:S(2)}) %collective-permute-start.31) | collective-permute-done | bytes 524320 | tf_op jit(solution)/shard_map/ppermute | solution.py:1299
  277.4 19.1 %collective-permute-done.32 = bf16[256,2048]{1,0:T(8,128)(2,1)S(1)} collective-permute-done((bf16[256,2048]{1,0:T(8,128)(2,1)S(1)}, bf16[256,2048]{1,0:T(8,128)(2,1)S(1)}, u32[]{:S(2)}, u32[]{:S(2)}) %collective-permute-start.32) | collective-permute-done | bytes 1048608 | tf_op jit(solution)/shard_map/ppermute | solution.py:1296
  300.5 7.5 %collective-permute-done.34 = bf16[128,2048]{1,0:T(8,128)(2,1)S(1)} collective-permute-done((bf16[128,2048]{1,0:T(8,128)(2,1)S(1)}, bf16[128,2048]{1,0:T(8,128)(2,1)S(1)}, u32[]{:S(2)}, u32[]{:S(2)}) %collective-permute-start.34) | collective-permute-done | bytes 524320 | tf_op jit(solution)/shard_map/ppermute | solution.py:1298
  312.7 16.7 %gate_up.1 = (bf16[1024,1408]{1,0:T(8,128)(2,1)S(1)}, bf16[1024,1408]{1,0:T(8,128)(2,1)S(1)}, bf16[1024,1408]{1,0:T(8,128)(2,1)S(1)}) custom-call(bf16[1024,2048]{1,0:T(8,128)(2,1)S(1)} %copy-done.34, bf16[2048,2816]{1,0:T(8,128)(2,1)} %all-gather.9.cloned.1.call-done.w_ref), custom_call_target="tpu_custom_call" | custom-call | flops 11811160064 | bytes 24379392 | tf_op jit(solution)/shard_map/gate_up/pallas_call | solution.py:1125
  334.2 8.5 %convolution_convert_fusion.2 = bf16[2048,1408]{1,0:T(8,128)(2,1)} fusion(bf16[1024,2048]{1,0:T(8,128)(2,1)S(1)} %copy-done.31, bf16[1024,1408]{1,0:T(8,128)(2,1)S(1)} %get-tuple-element.357), kind=kOutput, calls=%fused_computation.2 | convolution fusion | flops 5908463616 | bytes 12845056 | tf_op jit(solution)/shard_map/dot_general | solution.py:1277
  348.9 12.2 %gate_up_back.1 = bf16[1024,2816]{1,0:T(8,128)(2,1)} custom-call(bf16[1024,2048]{1,0:T(8,128)(2,1)S(1)} %copy-done.32, bf16[2048,1408]{1,0:T(8,128)(2,1)} %all-gather.11.cloned.1.call-done.w_ref, bf16[1024,1408]{1,0:T(8,128)(2,1)S(1)} %copy-done.48, bf16[1024,1408]{1,0:T(8,128)(2,1)S(1)} %copy-done.50), custom_call_target="tpu_custom_call" | custom-call | flops 5905580032 | bytes 21495808 | tf_op jit(solution)/shard_map/gate_up_back/pallas_call | solution.py:1160
  361.1 18.2 %convolution_convert_fusion.3.own_ref = bf16[1024,2048]{1,0:T(8,128)(2,1)} fusion(bf16[1024,2816]{1,0:T(8,128)(2,1)} %gate_up_back.1, bf16[2048,2816]{1,0:T(8,128)(2,1)} %all-gather.9.cloned.1.call-done.w_ref), kind=kOutput, calls=%fused_computation.3 | convolution fusion | flops 11813257216 | bytes 21495808 | tf_op jit(solution)/shard_map/dot_general | solution.py:1277
  379.3 15.2 %convolution_convert_fusion = bf16[2048,2816]{1,0:T(8,128)(2,1)} fusion(bf16[1024,2048]{1,0:T(8,128)(2,1)S(1)} %copy-done.35, bf16[1024,2816]{1,0:T(8,128)(2,1)S(1)} %copy-done.80), kind=kOutput, calls=%fused_computation | convolution fusion | flops 11816927232 | bytes 21495808 | tf_op jit(solution)/shard_map/dot_general | solution.py:1277
  398.7 9.5 %collective-permute-done.38 = bf16[128,2048]{1,0:T(8,128)(2,1)S(1)} collective-permute-done((bf16[128,2048]{1,0:T(8,128)(2,1)S(1)}, bf16[128,2048]{1,0:T(8,128)(2,1)S(1)}, u32[]{:S(2)}, u32[]{:S(2)}) %collective-permute-start.38) | collective-permute-done | bytes 524320 | tf_op jit(solution)/shard_map/ppermute | solution.py:1307
  412.1 10.9 %convolution_convert_fusion.5.own_ref = bf16[1024,2048]{1,0:T(8,128)(2,1)} fusion(bf16[1024,1408]{1,0:T(8,128)(2,1)S(1)} %copy-done.62, bf16[2048,1408]{1,0:T(8,128)(2,1)} %all-gather.11.cloned.1.call-done.w_ref), kind=kOutput, calls=%fused_computation.5 | convolution fusion | flops 5907677184 | bytes 12845056 | tf_op jit(solution)/shard_map/dot_general | solution.py:1277
  423.0 6.2 collective-permute-done.37.x_ref
  439.0 16.4 %collective-permute-done.40 = bf16[256,2048]{1,0:T(8,128)(2,1)} collective-permute-done((bf16[256,2048]{1,0:T(8,128)(2,1)S(1)}, bf16[256,2048]{1,0:T(8,128)(2,1)}, u32[]{:S(2)}, u32[]{:S(2)}) %collective-permute-start.40) | collective-permute-done | bytes 1048608 | tf_op jit(solution)/shard_map/ppermute | solution.py:1296
  461.7 18.0 %collective-permute-done.44 = bf16[2,128,1408]{2,1,0:T(8,128)(2,1)S(1)} collective-permute-done((bf16[2,128,1408]{2,1,0:T(8,128)(2,1)}, bf16[2,128,1408]{2,1,0:T(8,128)(2,1)S(1)}, u32[]{:S(2)}, u32[]{:S(2)}) %collective-permute-start.44) | collective-permute-done | bytes 720928 | tf_op jit(solution)/shard_map/ppermute | solution.py:1449
  491.0 7.4 %adam_down.1 = (f32[512,1408]{1,0:T(8,128)}, f32[512,1408]{1,0:T(8,128)}, f32[512,1408]{1,0:T(8,128)}) custom-call(s32[4]{0:T(128)S(1)} %compare_convert_fusion.keep_ref, f32[512,1408]{1,0:T(8,128)S(1)} %copy-done.10, f32[512,1408]{1,0:T(8,128)S(1)} %copy-done.24, f32[512,1408]{1,0:T(8,128)S(1)} %copy-done.25, bf16[4,128,1408]{2,1,0:T(8,128)(2,1)} %get-tuple-element.437.g_ref), custom_call_target="tpu_custom_call" | custom-call | flops 8650752 | bytes 18743296 | tf_op jit(solution)/shard_map/adam_down/pallas_call | solution.py:1208
  509.3 8.6 %collective-permute-done.49 = bf16[128,2048]{1,0:T(8,128)(2,1)} collective-permute-done((bf16[128,2048]{1,0:T(8,128)(2,1)}, bf16[128,2048]{1,0:T(8,128)(2,1)}, u32[]{:S(2)}, u32[]{:S(2)}) %collective-permute-start.49) | collective-permute-done | bytes 524320 | tf_op jit(solution)/shard_map/ppermute | solution.py:1307
  526.1 26.8 %attend_back.1 = (bf16[1024,1536]{1,0:T(8,128)(2,1)}, f32[8,1536]{1,0:T(8,128)S(1)}) custom-call(s32[1]{0:T(128)} %bitcast.9.row_ref, s32[1,2]{1,0:T(1,128)S(1)} %copy-done.40, bf16[1024,512]{1,0:T(8,128)(2,1)S(1)} %copy-done.56, bf16[1024,512]{1,0:T(8,128)(2,1)S(1)} %copy-done.58, bf16[1024,512]{1,0:T(8,128)(2,1)S(1)} %copy-done.60, ...), custom_call_target="tpu_custom_call" | custom-call | flops 17179869184 | bytes 10485760 | tf_op jit(solution)/shard_map/attend_back/pallas_call | solution.py:1081
  556.9 11.2 %convolution_convert_fusion.4.own_ref = bf16[1024,2048]{1,0:T(8,128)(2,1)} fusion(bf16[1024,1536]{1,0:T(8,128)(2,1)S(1)} %copy-done.81, bf16[2048,1536]{1,0:T(8,128)(2,1)} %all-gather.5.cloned.1.call-done), kind=kOutput, calls=%fused_computation.4 | convolution fusion | flops 6444548096 | bytes 13631488 | tf_op jit(solution)/shard_map/dot_general | solution.py:1277
  568.2 8.7 %convolution_convert_fusion.1 = bf16[2048,1536]{1,0:T(8,128)(2,1)} fusion(bf16[1024,2048]{1,0:T(8,128)(2,1)S(1)} %copy-done.19, bf16[1024,1536]{1,0:T(8,128)(2,1)S(1)} %copy-done.81), kind=kOutput, calls=%fused_computation.1 | convolution fusion | flops 6445596672 | bytes 13631488 | tf_op jit(solution)/shard_map/dot_general | solution.py:1277
  583.7 31.2 %collective-permute-done.55 = bf16[2,128,2816]{2,1,0:T(8,128)(2,1)S(1)} collective-permute-done((bf16[2,128,2816]{2,1,0:T(8,128)(2,1)}, bf16[2,128,2816]{2,1,0:T(8,128)(2,1)S(1)}, u32[]{:S(2)}, u32[]{:S(2)}) %collective-permute-start.55) | collective-permute-done | bytes 1441824 | tf_op jit(solution)/shard_map/ppermute | solution.py:1449
  628.0 12.5 %adam_gate.1 = (f32[11264,128]{1,0:T(8,128)}, f32[11264,128]{1,0:T(8,128)}, f32[11264,128]{1,0:T(8,128)}) custom-call(s32[4]{0:T(128)S(1)} %compare_convert_fusion.keep_ref, f32[11264,128]{1,0:T(8,128)S(1)} %bitcast.88, f32[11264,128]{1,0:T(8,128)S(1)} %bitcast.96, f32[11264,128]{1,0:T(8,128)} %bitcast.104, bf16[4,128,2816]{2,1,0:T(8,128)(2,1)} %get-tuple-element.438.g_ref), custom_call_target="tpu_custom_call" | custom-call | flops 17301504 | bytes 37486592 | tf_op jit(solution)/shard_map/adam_gate/pallas_call | solution.py:1208
  687.5 12.7 %collective-permute-done.66 = bf16[2,128,1536]{2,1,0:T(8,128)(2,1)S(1)} collective-permute-done((bf16[2,128,1536]{2,1,0:T(8,128)(2,1)}, bf16[2,128,1536]{2,1,0:T(8,128)(2,1)S(1)}, u32[]{:S(2)}, u32[]{:S(2)}) %collective-permute-start.66) | collective-permute-done | bytes 786464 | tf_op jit(solution)/shard_map/ppermute | solution.py:1449
  711.6 9.6 %adam_query.1 = (f32[3,512,512]{2,1,0:T(8,128)}, f32[3,512,512]{2,1,0:T(8,128)}, f32[3,512,512]{2,1,0:T(8,128)}) custom-call(s32[4]{0:T(128)S(1)} %compare_convert_fusion.keep_ref, f32[3,512,512]{2,1,0:T(8,128)S(1)} %bitcast.93, f32[3,512,512]{2,1,0:T(8,128)S(1)} %bitcast.97, f32[3,512,512]{2,1,0:T(8,128)S(1)} %bitcast.98, ...), custom_call_target="tpu_custom_call" | custom-call | flops 9437184 | bytes 20447232 | tf_op jit(solution)/shard_map/adam_query/pallas_call | solution.py:1208
  (376 shorter events, 303.6 us)
Async XLA Ops:
  7.2 112.3 %all-gather.5.cloned.1.call-start = ((), (), s32[]{:S(2)}) async-start(), calls=%async_computation.4 | async-start | bytes 7077888 | tf_op jit(solution)/shard_map/all_gather | solution.py:1442
  14.2 26.5 %collective-permute-start.13 = (bf16[256,2048]{1,0:T(8,128)(2,1)S(1)}, bf16[256,2048]{1,0:T(8,128)(2,1)}, u32[]{:S(2)}, u32[]{:S(2)}) collective-permute-start(bf16[256,2048]{1,0:T(8,128)(2,1)S(1)} %norm_one.1), channel_id=1, source_target_pairs={{0,16},{8,24},{16,0},{24,8},{1,17},{9,25},{17,1},{25,9},{2,18},{10... | collective-permute-start | bytes 3145736 | tf_op jit(solution)/shard_map/ppermute | solution.py:1297
  16.8 25.4 %collective-permute-start.12 = (bf16[256,2048]{1,0:T(8,128)(2,1)S(1)}, bf16[256,2048]{1,0:T(8,128)(2,1)}, u32[]{:S(2)}, u32[]{:S(2)}) collective-permute-start(bf16[256,2048]{1,0:T(8,128)(2,1)S(1)} %norm_one.1), channel_id=1, source_target_pairs={{0,8},{8,0},{16,24},{24,16},{1,9},{9,1},{17,25},{25,17},{2,10},{10... | collective-permute-start | bytes 3145736 | tf_op jit(solution)/shard_map/ppermute | solution.py:1296
  44.8 155.4 %all-gather.7.cloned.1.call-start = ((), (), s32[]{:S(2)}) async-start(), calls=%async_computation.5 | async-start | bytes 2359296 | tf_op jit(solution)/shard_map/all_gather | solution.py:1442
  47.4 38.9 %collective-permute-start.19 = (bf16[4,128,512]{2,1,0:T(8,128)(2,1)}, bf16[4,128,512]{2,1,0:T(8,128)(2,1)}, u32[]{:S(2)}, u32[]{:S(2)}) collective-permute-start(bf16[4,128,512]{2,1,0:T(8,128)(2,1)} %pack_output.1.refs_0_), channel_id=1, source_target_pairs={{0,1},{1,0},{2,3},{3,2},{4,5},{5,4},{6,7},{7,6},{8,9},{9,8},{10,11... | collective-permute-start | bytes 1572872 | tf_op jit(solution)/shard_map/ppermute | solution.py:1330
  52.3 56.9 %collective-permute-start.18 = (bf16[4,128,2816]{2,1,0:T(8,128)(2,1)}, bf16[4,128,2816]{2,1,0:T(8,128)(2,1)}, u32[]{:S(2)}, u32[]{:S(2)}) collective-permute-start(bf16[4,128,2816]{2,1,0:T(8,128)(2,1)} %pack_gate.1.refs_0_), channel_id=1, source_target_pairs={{0,1},{1,0},{2,3},{3,2},{4,5},{5,4},{6,7},{7,6},{8,9},{9,8},{10,11... | collective-permute-start | bytes 8650760 | tf_op jit(solution)/shard_map/ppermute | solution.py:1330
  103.8 206.7 %all-gather.9.cloned.1.call-start = ((), (), s32[]{:S(2)}) async-start(), calls=%async_computation.6 | async-start | bytes 12976128 | tf_op jit(solution)/shard_map/all_gather | solution.py:1442
  112.1 39.9 %collective-permute-start.21 = (bf16[2,128,2816]{2,1,0:T(8,128)(2,1)}, bf16[2,128,2816]{2,1,0:T(8,128)(2,1)}, u32[]{:S(2)}, u32[]{:S(2)}) collective-permute-start(bf16[2,128,2816]{2,1,0:T(8,128)(2,1)} %pick_blocks.46), channel_id=1, source_target_pairs={{0,2},{2,4},{3,1},{4,6},{5,3},{7,5},{8,10},{10,12},{11,9},{12,14},... | collective-permute-start | bytes 4325384 | tf_op jit(solution)/shard_map/ppermute | solution.py:1430
  155.1 188.0 %all-gather.11.cloned.1.call-start = ((), (), s32[]{:S(2)}) async-start(), calls=%async_computation.7 | async-start | bytes 6488064 | tf_op jit(solution)/shard_map/all_gather | solution.py:1442
  162.6 31.3 %collective-permute-start.27 = (bf16[2,128,1408]{2,1,0:T(8,128)(2,1)S(1)}, bf16[2,128,1408]{2,1,0:T(8,128)(2,1)S(1)}, u32[]{:S(2)}, u32[]{:S(2)}) collective-permute-start(bf16[2,128,1408]{2,1,0:T(8,128)(2,1)S(1)} %pick_blocks.47), channel_id=1, source_target_pairs={{0,2},{2,4},{3,1},{4,6},{5,3},{7,5},{8,10},{10,12},{11,9},{12,14},... | collective-permute-start | bytes 2162696 | tf_op jit(solution)/shard_map/ppermute | solution.py:1430
  195.7 241.5 %reduce-scatter.5.cloned.1.call-start = ((), (), s32[]{:S(2)}) async-start(), calls=%async_computation.8 | async-start | bytes 6488064 | tf_op jit(solution)/shard_map/reduce_scatter | solution.py:1445
  198.5 26.3 %collective-permute-start.28 = (bf16[256,2048]{1,0:T(8,128)(2,1)S(1)}, bf16[256,2048]{1,0:T(8,128)(2,1)}, u32[]{:S(2)}, u32[]{:S(2)}) collective-permute-start(bf16[256,2048]{1,0:T(8,128)(2,1)S(1)} %order_grad.1), channel_id=1, source_target_pairs={{0,8},{8,0},{16,24},{24,16},{1,9},{9,1},{17,25},{25,17},{2,10},{10... | collective-permute-start | bytes 3145736 | tf_op jit(solution)/shard_map/ppermute | solution.py:1296
  204.7 28.0 %collective-permute-start.24 = (bf16[128,2048]{1,0:T(8,128)(2,1)S(1)}, bf16[128,2048]{1,0:T(8,128)(2,1)S(1)}, u32[]{:S(2)}, u32[]{:S(2)}) collective-permute-start(bf16[128,2048]{1,0:T(8,128)(2,1)S(1)} %get-tuple-element.425), channel_id=1, source_target_pairs={{0,8},{8,0},{16,24},{24,16},{1,9},{9,1},{17,25},{25,17},{2,10},{10... | collective-permute-start | bytes 1572872 | tf_op jit(solution)/shard_map/ppermute | solution.py:1307
  205.1 27.6 %collective-permute-start.22 = (bf16[128,2048]{1,0:T(8,128)(2,1)S(1)}, bf16[128,2048]{1,0:T(8,128)(2,1)S(1)}, u32[]{:S(2)}, u32[]{:S(2)}) collective-permute-start(bf16[128,2048]{1,0:T(8,128)(2,1)S(1)} %get-tuple-element.427), channel_id=1, source_target_pairs={{0,16},{8,24},{16,0},{24,8},{1,17},{9,25},{17,1},{25,9},{2,18},{10... | collective-permute-start | bytes 1572872 | tf_op jit(solution)/shard_map/ppermute | solution.py:1306
  206.8 35.6 %collective-permute-start.29 = (bf16[256,2048]{1,0:T(8,128)(2,1)S(1)}, bf16[256,2048]{1,0:T(8,128)(2,1)S(1)}, u32[]{:S(2)}, u32[]{:S(2)}) collective-permute-start(bf16[256,2048]{1,0:T(8,128)(2,1)S(1)} %order_grad.1), channel_id=1, source_target_pairs={{0,16},{8,24},{16,0},{24,8},{1,17},{9,25},{17,1},{25,9},{2,18},{10... | collective-permute-start | bytes 3145736 | tf_op jit(solution)/shard_map/ppermute | solution.py:1297
  225.8 27.8 %collective-permute-start.30 = (bf16[128,2048]{1,0:T(8,128)(2,1)S(1)}, bf16[128,2048]{1,0:T(8,128)(2,1)S(1)}, u32[]{:S(2)}, u32[]{:S(2)}) collective-permute-start(bf16[128,2048]{1,0:T(8,128)(2,1)S(1)} %slice.136), channel_id=1, source_target_pairs={{0,16},{8,24},{16,0},{24,8},{1,17},{9,25},{17,1},{25,9},{2,18},{10... | collective-permute-start | bytes 1572872 | tf_op jit(solution)/shard_map/ppermute | solution.py:1298
  232.9 33.5 %collective-permute-start.23 = (bf16[256,2048]{1,0:T(8,128)(2,1)S(1)}, bf16[256,2048]{1,0:T(8,128)(2,1)S(1)}, u32[]{:S(2)}, u32[]{:S(2)}) collective-permute-start(bf16[256,2048]{1,0:T(8,128)(2,1)S(1)} %pad_maximum_fusion), channel_id=1, source_target_pairs={{0,8},{8,0},{16,24},{24,16},{1,9},{9,1},{17,25},{25,17},{2,10},{10... | collective-permute-start | bytes 3145736 | tf_op jit(solution)/shard_map/ppermute | solution.py:1313
  234.7 37.6 %collective-permute-start.25 = (bf16[256,2048]{1,0:T(8,128)(2,1)S(1)}, bf16[256,2048]{1,0:T(8,128)(2,1)S(1)}, u32[]{:S(2)}, u32[]{:S(2)}) collective-permute-start(bf16[256,2048]{1,0:T(8,128)(2,1)S(1)} %pad_maximum_fusion.1), channel_id=1, source_target_pairs={{0,16},{8,24},{16,0},{24,8},{1,17},{9,25},{17,1},{25,9},{2,18},{10... | collective-permute-start | bytes 3145736 | tf_op jit(solution)/shard_map/ppermute | solution.py:1313
  242.4 23.9 %collective-permute-start.31 = (bf16[128,2048]{1,0:T(8,128)(2,1)S(1)}, bf16[128,2048]{1,0:T(8,128)(2,1)S(1)}, u32[]{:S(2)}, u32[]{:S(2)}) collective-permute-start(bf16[128,2048]{1,0:T(8,128)(2,1)S(1)} %slice.137), channel_id=1, source_target_pairs={{0,8},{8,0},{16,24},{24,16},{1,9},{9,1},{17,25},{25,17},{2,10},{10... | collective-permute-start | bytes 1572872 | tf_op jit(solution)/shard_map/ppermute | solution.py:1299
  342.8 234.1 %reduce-scatter.11.cloned.1.call-start = ((), (), s32[]{:S(2)}) async-start(), calls=%async_computation.11 | async-start | bytes 12976128 | tf_op jit(solution)/shard_map/reduce_scatter | solution.py:1445
  394.5 245.9 %reduce-scatter.9.cloned.1.call-start = ((), (), s32[]{:S(2)}) async-start(), calls=%async_computation.10 | async-start | bytes 2359296 | tf_op jit(solution)/shard_map/reduce_scatter | solution.py:1445
  437.1 42.5 %collective-permute-start.44 = (bf16[2,128,1408]{2,1,0:T(8,128)(2,1)}, bf16[2,128,1408]{2,1,0:T(8,128)(2,1)S(1)}, u32[]{:S(2)}, u32[]{:S(2)}) collective-permute-start(bf16[2,128,1408]{2,1,0:T(8,128)(2,1)} %bitcast.115), channel_id=1, source_target_pairs={{1,3},{2,0},{3,5},{4,2},{5,7},{6,4},{9,11},{10,8},{11,13},{12,10},... | collective-permute-start | bytes 2162696 | tf_op jit(solution)/shard_map/ppermute | solution.py:1449
  456.5 24.6 %collective-permute-start.42 = (bf16[128,2048]{1,0:T(8,128)(2,1)S(1)}, bf16[128,2048]{1,0:T(8,128)(2,1)S(1)}, u32[]{:S(2)}, u32[]{:S(2)}) collective-permute-start(bf16[128,2048]{1,0:T(8,128)(2,1)S(1)} %slice.146), channel_id=1, source_target_pairs={{0,16},{8,24},{16,0},{24,8},{1,17},{9,25},{17,1},{25,9},{2,18},{10... | collective-permute-start | bytes 1572872 | tf_op jit(solution)/shard_map/ppermute | solution.py:1298
  509.0 177.1 %reduce-scatter.7.cloned.1.call-start = ((), (), s32[]{:S(2)}) async-start(), calls=%async_computation.9 | async-start | bytes 7077888 | tf_op jit(solution)/shard_map/reduce_scatter | solution.py:1445
  521.6 31.4 %collective-permute-start.48 = (bf16[256,2048]{1,0:T(8,128)(2,1)}, bf16[256,2048]{1,0:T(8,128)(2,1)S(1)}, u32[]{:S(2)}, u32[]{:S(2)}) collective-permute-start(bf16[256,2048]{1,0:T(8,128)(2,1)} %pad_maximum_fusion.4), channel_id=1, source_target_pairs={{0,8},{8,0},{16,24},{24,16},{1,9},{9,1},{17,25},{25,17},{2,10},{10... | collective-permute-start | bytes 3145736 | tf_op jit(solution)/shard_map/ppermute | solution.py:1313
  525.5 27.5 %collective-permute-start.50 = (bf16[256,2048]{1,0:T(8,128)(2,1)}, bf16[256,2048]{1,0:T(8,128)(2,1)}, u32[]{:S(2)}, u32[]{:S(2)}) collective-permute-start(bf16[256,2048]{1,0:T(8,128)(2,1)} %pad_maximum_fusion.5), channel_id=1, source_target_pairs={{0,16},{8,24},{16,0},{24,8},{1,17},{9,25},{17,1},{25,9},{2,18},{10... | collective-permute-start | bytes 3145736 | tf_op jit(solution)/shard_map/ppermute | solution.py:1313
  576.9 38.0 %collective-permute-start.55 = (bf16[2,128,2816]{2,1,0:T(8,128)(2,1)}, bf16[2,128,2816]{2,1,0:T(8,128)(2,1)S(1)}, u32[]{:S(2)}, u32[]{:S(2)}) collective-permute-start(bf16[2,128,2816]{2,1,0:T(8,128)(2,1)} %bitcast.105), channel_id=1, source_target_pairs={{1,3},{2,0},{3,5},{4,2},{5,7},{6,4},{9,11},{10,8},{11,13},{12,10},... | collective-permute-start | bytes 4325384 | tf_op jit(solution)/shard_map/ppermute | solution.py:1449
  580.2 34.6 %collective-permute-start.53 = (bf16[128,2048]{1,0:T(8,128)(2,1)S(1)}, bf16[128,2048]{1,0:T(8,128)(2,1)S(1)}, u32[]{:S(2)}, u32[]{:S(2)}) collective-permute-start(bf16[128,2048]{1,0:T(8,128)(2,1)S(1)} %get-tuple-element.407), channel_id=1, source_target_pairs={{0,8},{8,0},{16,24},{24,16},{1,9},{9,1},{17,25},{25,17},{2,10},{10... | collective-permute-start | bytes 1572872 | tf_op jit(solution)/shard_map/ppermute | solution.py:1307
  581.6 33.3 %collective-permute-start.51 = (bf16[128,2048]{1,0:T(8,128)(2,1)S(1)}, bf16[128,2048]{1,0:T(8,128)(2,1)S(1)}, u32[]{:S(2)}, u32[]{:S(2)}) collective-permute-start(bf16[128,2048]{1,0:T(8,128)(2,1)S(1)} %get-tuple-element.409), channel_id=1, source_target_pairs={{0,16},{8,24},{16,0},{24,8},{1,17},{9,25},{17,1},{25,9},{2,18},{10... | collective-permute-start | bytes 1572872 | tf_op jit(solution)/shard_map/ppermute | solution.py:1306
  582.0 37.1 %collective-permute-start.56 = (bf16[2,128,2816]{2,1,0:T(8,128)(2,1)S(1)}, bf16[2,128,2816]{2,1,0:T(8,128)(2,1)S(1)}, u32[]{:S(2)}, u32[]{:S(2)}) collective-permute-start(bf16[2,128,2816]{2,1,0:T(8,128)(2,1)S(1)} %bitcast.106), channel_id=1, source_target_pairs={{0,1},{1,0},{2,3},{3,2},{4,5},{5,4},{6,7},{7,6},{8,9},{9,8},{10,11... | collective-permute-start | bytes 4325384 | tf_op jit(solution)/shard_map/ppermute | solution.py:1330
  617.2 25.8 %collective-permute-start.52 = (bf16[256,2048]{1,0:T(8,128)(2,1)}, bf16[256,2048]{1,0:T(8,128)(2,1)S(1)}, u32[]{:S(2)}, u32[]{:S(2)}) collective-permute-start(bf16[256,2048]{1,0:T(8,128)(2,1)} %pad_maximum_fusion.6), channel_id=1, source_target_pairs={{0,8},{8,0},{16,24},{24,16},{1,9},{9,1},{17,25},{25,17},{2,10},{10... | collective-permute-start | bytes 3145736 | tf_op jit(solution)/shard_map/ppermute | solution.py:1313
  618.6 25.6 %collective-permute-start.54 = (bf16[256,2048]{1,0:T(8,128)(2,1)}, bf16[256,2048]{1,0:T(8,128)(2,1)}, u32[]{:S(2)}, u32[]{:S(2)}) collective-permute-start(bf16[256,2048]{1,0:T(8,128)(2,1)} %pad_maximum_fusion.7), channel_id=1, source_target_pairs={{0,16},{8,24},{16,0},{24,8},{1,17},{9,25},{17,1},{25,9},{2,18},{10... | collective-permute-start | bytes 3145736 | tf_op jit(solution)/shard_map/ppermute | solution.py:1313
  (109 other events, 1150.3 us)
Sparse Core Ops, SparseCore 0:
  44.9 68.6 all-gather.4
  115.8 32.9 all-gather.6
  155.2 116.6 all-gather.8
  273.9 62.4 all-gather.10
  342.9 72.7 reduce-scatter.4
  417.8 125.3 reduce-scatter.10
  546.1 34.1 reduce-scatter.8
  582.6 81.2 reduce-scatter.6
